TPU v7x, 32 devices: a whole 2x2x4 slice. The times are simulated.
32 devices in a mesh: gx: 4 (over x, core), gy: 2 (over y), gz: 4 (over z).
Axes of the slice: x: 2, y: 2, z: 4, core: 2. Of those that a mesh axis runs over, the one named last changes fastest.
Arguments:
- phase: int32 [256, 16, 512], P('gx', 'gy', 'gz'), may hold values from 0 to 2
- perm_scale: float32 [256, 16, 512], P('gx', 'gy', 'gz'), may hold values from 0.5 to 2
- magnetization: bfloat16 [3, 256, 16, 512], P(None, 'gx', 'gy', 'gz'), may hold values from -4 to 4
- stiffness: float32 [256, 16, 512], P(('gx', 'gy'), None, 'gz'), may hold values from 0.5 to 4
Outputs:
- strain: bfloat16 [6, 256, 16, 512], P(None, 'gx', 'gy', 'gz')
All inputs are finite; a program needn't handle non-finite values.
Results may differ from a plain program's by a relative error of at most 0.001.
The roundings to bfloat16 on the way count: a program that leaves them out, or rounds other values in their place, can miss the bound.
Values may be sent and summed in bfloat16 or wider, within the bound.
A program may use at most 64 MiB of HBM per device.

v0:
```python
import math
import jax
import jax.numpy as jnp
from jax import lax
from jax.sharding import PartitionSpec as P

SWEEPS = 3
STRAIN_PAIRS = ((0, 0), (1, 1), (2, 2), (0, 1), (1, 2), (0, 2))
MAGNETO = 4.0


def padded_2(value, sides, width):
    for axis, dim in sides:
        devices, length = (lax.axis_size(axis), value.shape[dim])
        up = [(i, (i + 1) % devices) for i in range(devices - 1)]
        down = [(j, i) for i, j in up]
        last = lax.slice_in_dim(value, length - width, length, axis=dim)
        leading = lax.slice_in_dim(value, 0, width, axis=dim)
        before = lax.ppermute(last, axis, up)
        after = lax.ppermute(leading, axis, down)
        value = jnp.concatenate([before, value, after], axis=dim)
    return value


def chebyshev_weights(middle, radius, count):
    return [
        1.0 / (middle + radius * math.cos((2 * counter + 1) * math.pi / (2 * count)))
        for counter in range(count)
    ]


def unit_offset(dimension, sign):
    offsets = [0, 0, 0]
    offsets[dimension] = sign
    return offsets


def window(padded, offsets):
    shape = padded.shape[-3:]
    selection = tuple(
        (slice(1 + moved, extent - 1 + moved) for moved, extent in zip(offsets, shape))
    )
    leading = tuple((slice(None) for counter in range(padded.ndim - 3)))
    return padded[leading + selection]


def central(padded, dimension):
    return (
        window(padded, unit_offset(dimension, 1)) - window(padded, unit_offset(dimension, -1))
    ) * 0.5


def neighbours(padded):
    total = window(padded, unit_offset(0, 1)) + window(padded, unit_offset(0, -1))
    for dimension in (1, 2):
        total = (
            total
            + window(padded, unit_offset(dimension, 1))
            + window(padded, unit_offset(dimension, -1))
        )
    return total


def magnet_force(moments_pad, potential_pad):
    total = [moments_pad[dimension] - central(potential_pad, dimension) for dimension in range(3)]
    inner = moments_pad[0] * total[0] + moments_pad[1] * total[1] + moments_pad[2] * total[2]
    stress = {}
    for first, second in STRAIN_PAIRS:
        value = 0.5 * (moments_pad[first] * total[second] + moments_pad[second] * total[first])
        if first == second:
            value = value - inner / 3.0
        stress[first, second] = MAGNETO * value
        stress[second, first] = stress[first, second]
    force = []
    for first in range(3):
        acc = central(stress[first, 0], 0)
        for second in (1, 2):
            acc = acc + central(stress[first, second], second)
        force.append(acc)
    return jnp.stack(force)


def navier(padded):
    result = []
    for first in range(3):
        center = window(padded[first], [0, 0, 0])
        value = 6.0 * center - neighbours(padded[first])
        second_diff = (
            window(padded[first], unit_offset(first, 1))
            - 2.0 * center
            + window(padded[first], unit_offset(first, -1))
        )
        for second in range(3):
            if second != first:
                plus_plus = [0, 0, 0]
                plus_plus[first] = 1
                plus_plus[second] = 1
                plus_minus = [0, 0, 0]
                plus_minus[first] = 1
                plus_minus[second] = -1
                minus_plus = [0, 0, 0]
                minus_plus[first] = -1
                minus_plus[second] = 1
                minus_minus = [0, 0, 0]
                minus_minus[first] = -1
                minus_minus[second] = -1
                second_diff = second_diff + 0.25 * (
                    window(padded[second], plus_plus)
                    - window(padded[second], plus_minus)
                    - window(padded[second], minus_plus)
                    + window(padded[second], minus_minus)
                )
        result.append(value - second_diff)
    return jnp.stack(result)


def strain_from(padded):
    result = []
    for first, second in STRAIN_PAIRS:
        result.append(0.5 * (central(padded[second], first) + central(padded[first], second)))
    return jnp.stack(result)


def potential_rim(field):
    return padded_2(field, (("gx", 0), ("gy", 1), ("gz", 2)), 2)


def elastic_solve(load, modulus, pad_field):
    elastic_weights = chebyshev_weights(1.3, 1.2, SWEEPS)
    elastic_diag = 8.0 * modulus
    displacement = elastic_weights[0] * load / elastic_diag
    for counter in range(1, SWEEPS):
        padded = pad_field(displacement)
        displacement = (
            displacement
            + elastic_weights[counter] * (load - modulus * navier(padded)) / elastic_diag
        )
    return displacement


def per_device(phase, perm_scale, magnetization, stiffness):
    magnetic = phase == 0
    permeability = (
        jnp.where(magnetic, 4.0, jnp.where(phase == 1, 1.5, 1.0)).astype(jnp.float32) * perm_scale
    )
    moments = magnetization * magnetic.astype(jnp.bfloat16)[None]
    moments_pad = padded_2(moments, (("gx", 1), ("gy", 2), ("gz", 3)), 1).astype(jnp.float32)
    source = -(central(moments_pad[0], 0) + central(moments_pad[1], 1) + central(moments_pad[2], 2))
    weights = chebyshev_weights(1.0, 0.9, SWEEPS)
    diagonal = 6.0 * permeability
    potential = weights[0] * source / diagonal
    for counter in range(1, SWEEPS):
        padded = potential_rim(potential)[1:-1, 1:-1, 1:-1]
        potential = (
            potential
            + weights[counter]
            * (source - permeability * (6.0 * potential - neighbours(padded)))
            / diagonal
        )
    force = magnet_force(moments_pad, potential_rim(potential)).astype(jnp.bfloat16)
    load = lax.all_to_all(force, "gy", split_axis=1, concat_axis=2, tiled=True).astype(jnp.float32)

    def pad_slab(field):
        rimmed = padded_2(field, ((("gx", "gy"), 1), ("gz", 3)), 1)
        return jnp.pad(rimmed, ((0, 0), (0, 0), (1, 1), (0, 0)))

    displacement = elastic_solve(load, stiffness, pad_slab)
    strain = strain_from(pad_slab(displacement)).astype(jnp.bfloat16)
    return lax.all_to_all(strain, "gy", split_axis=2, concat_axis=1, tiled=True)


def solution(mesh):
    placed = (
        P("gx", "gy", "gz"),
        P("gx", "gy", "gz"),
        P(None, "gx", "gy", "gz"),
        P(("gx", "gy"), None, "gz"),
    )
    return jax.shard_map(
        per_device, mesh=mesh, in_specs=placed, out_specs=P(None, "gx", "gy", "gz"), check_vma=False
    )
```

profile of v0, /device:TPU:0, one launch (start us, length us, event | category | flops | bytes accessed | tf_op | source)
XLA Modules:
  0.0 224.6 jit_solution(4618047857174763802)
XLA Ops:
  2.4 2.4 %collective-permute-start = (bf16[3,1,8,128]{3,2,1,0:T(8,128)(2,1)S(1)}, bf16[3,1,8,128]{3,2,1,0:T(8,128)(2,1)S(1)}, u32[]{:S(2)}, u32[]{:S(2)}) collective-permute-start(bf16[3,1,8,128]{3,2,1,0:T(8,128)(2,1)S(1)} %get-tuple-element.66), channel_id=1, source_target_pairs={{0,8},{8,16},{16,24},{1,9},{9,17},{17,25},{2,10},{10,18},{18,26},{... | collective-permute-start | bytes 18440 | tf_op jit(solution)/shard_map/ppermute | solution.py:19
  4.8 1.3 collective-permute-start.1
  6.1 3.9 %collective-permute-done.1 = bf16[3,1,8,128]{3,2,1,0:T(8,128)(2,1)S(1)} collective-permute-done((bf16[3,1,8,128]{3,2,1,0:T(8,128)(2,1)S(1)}, bf16[3,1,8,128]{3,2,1,0:T(8,128)(2,1)S(1)}, u32[]{:S(2)}, u32[]{:S(2)}) %collective-permute-start.1) | collective-permute-done | bytes 6176 | tf_op jit(solution)/shard_map/ppermute | solution.py:20
  10.5 3.4 %collective-permute-start.2 = (bf16[3,66,1,128]{1,3,2,0:T(8,128)(2,1)S(1)}, bf16[3,66,1,128]{1,3,2,0:T(8,128)(2,1)S(1)}, u32[]{:S(2)}, u32[]{:S(2)}) collective-permute-start(bf16[3,66,1,128]{1,3,2,0:T(8,128)(2,1)S(1)} %get-tuple-element.55), channel_id=1, source_target_pairs={{0,4},{1,5},{2,6},{3,7},{8,12},{9,13},{10,14},{11,15},{16,20},{17,... | collective-permute-start | bytes 152072 | tf_op jit(solution)/shard_map/ppermute | solution.py:19
  16.1 4.3 %collective-permute-done.3 = bf16[3,66,1,128]{1,3,2,0:T(8,128)(2,1)S(1)} collective-permute-done((bf16[3,66,1,128]{1,3,2,0:T(8,128)(2,1)S(1)}, bf16[3,66,1,128]{1,3,2,0:T(8,128)(2,1)S(1)}, u32[]{:S(2)}, u32[]{:S(2)}) %collective-permute-start.3) | collective-permute-done | bytes 50720 | tf_op jit(solution)/shard_map/ppermute | solution.py:20
  20.5 3.5 %collective-permute-start.4 = (bf16[3,66,10,1]{1,0,3,2:T(4,128)(2,1)S(1)}, bf16[3,66,10,1]{1,0,3,2:T(4,128)(2,1)S(1)}, u32[]{:S(2)}, u32[]{:S(2)}) collective-permute-start(bf16[3,66,10,1]{1,0,3,2:T(4,128)(2,1)S(1)} %copy.93), channel_id=1, source_target_pairs={{0,1},{1,2},{2,3},{4,5},{5,6},{6,7},{8,9},{9,10},{10,11},{12,13},{... | collective-permute-start | bytes 11888 | tf_op jit(solution)/shard_map/ppermute | solution.py:19
  25.6 4.0 %collective-permute-done.5 = bf16[3,66,10,1]{1,0,3,2:T(4,128)(2,1)S(1)} collective-permute-done((bf16[3,66,10,1]{1,0,3,2:T(4,128)(2,1)S(1)}, bf16[3,66,10,1]{1,0,3,2:T(4,128)(2,1)S(1)}, u32[]{:S(2)}, u32[]{:S(2)}) %collective-permute-start.5) | collective-permute-done | bytes 3992 | tf_op jit(solution)/shard_map/ppermute | solution.py:20
  32.3 3.1 %collective-permute-start.7 = (f32[2,8,128]{0,2,1:T(8,128)S(1)}, f32[2,8,128]{0,2,1:T(8,128)S(1)}, u32[]{:S(2)}, u32[]{:S(2)}) collective-permute-start(f32[2,8,128]{0,2,1:T(8,128)S(1)} %get-tuple-element.64), channel_id=1, source_target_pairs={{0,8},{8,16},{16,24},{1,9},{9,17},{17,25},{2,10},{10,18},{18,26},{... | collective-permute-start | bytes 24584 | tf_op jit(solution)/shard_map/ppermute | solution.py:19
  35.4 1.5 collective-permute-done.7
  38.4 4.6 %collective-permute-start.9 = (f32[68,2,128]{0,2,1:T(8,128)S(1)}, f32[68,2,128]{0,2,1:T(8,128)S(1)}, u32[]{:S(2)}, u32[]{:S(2)}) collective-permute-start(f32[68,2,128]{0,2,1:T(8,128)S(1)} %get-tuple-element.39), channel_id=1, source_target_pairs={{0,4},{1,5},{2,6},{3,7},{8,12},{9,13},{10,14},{11,15},{16,20},{17,... | collective-permute-start | bytes 208904 | tf_op jit(solution)/shard_map/ppermute | solution.py:19
  44.0 1.5 collective-permute-done.9
  45.6 1.3 collective-permute-start.10
  46.9 4.5 %collective-permute-start.11 = (f32[68,12,2]{0,2,1:T(2,128)S(1)}, f32[68,12,2]{0,2,1:T(2,128)S(1)}, u32[]{:S(2)}, u32[]{:S(2)}) collective-permute-start(f32[68,12,2]{0,2,1:T(2,128)S(1)} %get-tuple-element.34), channel_id=1, source_target_pairs={{0,1},{1,2},{2,3},{4,5},{5,6},{6,7},{8,9},{9,10},{10,11},{12,13},{... | collective-permute-start | bytes 19592 | tf_op jit(solution)/shard_map/ppermute | solution.py:19
  51.4 1.4 collective-permute-done.11
  52.8 1.7 fusion.45
  56.0 6.8 %collective-permute-start.13 = (f32[2,8,128]{0,2,1:T(8,128)S(1)}, f32[2,8,128]{0,2,1:T(8,128)S(1)}, u32[]{:S(2)}, u32[]{:S(2)}) collective-permute-start(f32[2,8,128]{0,2,1:T(8,128)S(1)} %get-tuple-element.62), channel_id=1, source_target_pairs={{0,8},{8,16},{16,24},{1,9},{9,17},{17,25},{2,10},{10,18},{18,26},{... | collective-permute-start | bytes 24584 | tf_op jit(solution)/shard_map/ppermute | solution.py:19
  62.8 1.5 collective-permute-done.13
  65.8 4.6 %collective-permute-start.15 = (f32[68,2,128]{0,2,1:T(8,128)S(1)}, f32[68,2,128]{0,2,1:T(8,128)S(1)}, u32[]{:S(2)}, u32[]{:S(2)}) collective-permute-start(f32[68,2,128]{0,2,1:T(8,128)S(1)} %get-tuple-element.37), channel_id=1, source_target_pairs={{0,4},{1,5},{2,6},{3,7},{8,12},{9,13},{10,14},{11,15},{16,20},{17,... | collective-permute-start | bytes 208904 | tf_op jit(solution)/shard_map/ppermute | solution.py:19
  71.4 1.5 collective-permute-done.15
  74.3 4.5 %collective-permute-start.17 = (f32[68,12,2]{0,2,1:T(2,128)S(1)}, f32[68,12,2]{0,2,1:T(2,128)S(1)}, u32[]{:S(2)}, u32[]{:S(2)}) collective-permute-start(f32[68,12,2]{0,2,1:T(2,128)S(1)} %get-tuple-element.32), channel_id=1, source_target_pairs={{0,1},{1,2},{2,3},{4,5},{5,6},{6,7},{8,9},{9,10},{10,11},{12,13},{... | collective-permute-start | bytes 19592 | tf_op jit(solution)/shard_map/ppermute | solution.py:19
  78.9 1.4 collective-permute-done.17
  80.2 1.7 fusion.35
  82.1 9.6 %collective-permute-start.18 = (f32[2,8,128]{0,2,1:T(8,128)S(1)}, f32[2,8,128]{0,2,1:T(8,128)S(1)}, u32[]{:S(2)}, u32[]{:S(2)}) collective-permute-start(f32[2,8,128]{0,2,1:T(8,128)S(1)} %get-tuple-element.60), channel_id=1, source_target_pairs={{0,8},{8,16},{16,24},{1,9},{9,17},{17,25},{2,10},{10,18},{18,26},{... | collective-permute-start | bytes 24584 | tf_op jit(solution)/shard_map/ppermute | solution.py:19
  93.3 6.2 %collective-permute-done.19 = f32[2,8,128]{0,2,1:T(8,128)S(1)} collective-permute-done((f32[2,8,128]{0,2,1:T(8,128)S(1)}, f32[2,8,128]{0,2,1:T(8,128)S(1)}, u32[]{:S(2)}, u32[]{:S(2)}) %collective-permute-start.19) | collective-permute-done | bytes 8224 | tf_op jit(solution)/shard_map/ppermute | solution.py:20
  99.6 4.4 %collective-permute-start.20 = (f32[68,2,128]{0,2,1:T(8,128)S(1)}, f32[68,2,128]{0,2,1:T(8,128)S(1)}, u32[]{:S(2)}, u32[]{:S(2)}) collective-permute-start(f32[68,2,128]{0,2,1:T(8,128)S(1)} %get-tuple-element.35), channel_id=1, source_target_pairs={{0,4},{1,5},{2,6},{3,7},{8,12},{9,13},{10,14},{11,15},{16,20},{17,... | collective-permute-start | bytes 208904 | tf_op jit(solution)/shard_map/ppermute | solution.py:19
  106.5 4.4 %collective-permute-done.21 = f32[68,2,128]{0,2,1:T(8,128)S(1)} collective-permute-done((f32[68,2,128]{0,2,1:T(8,128)S(1)}, f32[68,2,128]{0,2,1:T(8,128)S(1)}, u32[]{:S(2)}, u32[]{:S(2)}) %collective-permute-start.21) | collective-permute-done | bytes 69664 | tf_op jit(solution)/shard_map/ppermute | solution.py:20
  111.0 4.2 %collective-permute-start.22 = (f32[68,12,2]{0,2,1:T(2,128)S(1)}, f32[68,12,2]{0,2,1:T(2,128)S(1)}, u32[]{:S(2)}, u32[]{:S(2)}) collective-permute-start(f32[68,12,2]{0,2,1:T(2,128)S(1)} %get-tuple-element.29), channel_id=1, source_target_pairs={{0,1},{1,2},{2,3},{4,5},{5,6},{6,7},{8,9},{9,10},{10,11},{12,13},{... | collective-permute-start | bytes 19592 | tf_op jit(solution)/shard_map/ppermute | solution.py:19
  115.2 1.5 collective-permute-start.23
  116.7 4.1 %collective-permute-done.23 = f32[68,12,2]{0,2,1:T(2,128)S(1)} collective-permute-done((f32[68,12,2]{0,2,1:T(2,128)S(1)}, f32[68,12,2]{0,2,1:T(2,128)S(1)}, u32[]{:S(2)}, u32[]{:S(2)}) %collective-permute-start.23) | collective-permute-done | bytes 6560 | tf_op jit(solution)/shard_map/ppermute | solution.py:20
  121.1 1.6 subtract_multiply_fusion.2
  123.2 2.1 fusion.123
  126.6 3.5 %all-to-all-start = ((bf16[3,64,8,128]{3,2,0,1:T(8,128)(2,1)}), bf16[3,64,8,128]{3,2,0,1:T(8,128)(2,1)S(1)}, u32[]{:S(2)}, u32[]{:S(2)}) async-start(bf16[3,64,8,128]{3,2,0,1:T(8,128)(2,1)} %copy.99), calls=%async_computation | async-start | bytes 786432 | tf_op jit(solution)/shard_map/all_to_all | solution.py:161
  130.1 5.8 %all-to-all-done = bf16[3,64,8,128]{3,2,0,1:T(8,128)(2,1)S(1)} async-done(((bf16[3,64,8,128]{3,2,0,1:T(8,128)(2,1)}), bf16[3,64,8,128]{3,2,0,1:T(8,128)(2,1)S(1)}, u32[]{:S(2)}, u32[]{:S(2)}) %all-to-all-start) | async-done | bytes 393248 | tf_op jit(solution)/shard_map/all_to_all | solution.py:161
  136.2 1.9 collective-permute-start.24
  139.6 7.3 %collective-permute-done.25 = f32[3,1,16,128]{3,2,1,0:T(8,128)S(1)} collective-permute-done((f32[3,1,16,128]{3,2,1,0:T(8,128)S(1)}, f32[3,1,16,128]{3,2,1,0:T(8,128)S(1)}, u32[]{:S(2)}, u32[]{:S(2)}) %collective-permute-start.25) | collective-permute-done | bytes 24608 | tf_op jit(solution)/shard_map/ppermute | solution.py:20
  147.7 3.6 %collective-permute-start.26 = (f32[3,34,16,1]{1,2,3,0:T(8,128)S(1)}, f32[3,34,16,1]{1,2,3,0:T(8,128)S(1)}, u32[]{:S(2)}, u32[]{:S(2)}) collective-permute-start(f32[3,34,16,1]{1,2,3,0:T(8,128)S(1)} %copy.102), channel_id=1, source_target_pairs={{0,1},{1,2},{2,3},{4,5},{5,6},{6,7},{8,9},{9,10},{10,11},{12,13},{... | collective-permute-start | bytes 19592 | tf_op jit(solution)/shard_map/ppermute | solution.py:19
  153.6 3.9 %collective-permute-done.27 = f32[3,34,16,1]{1,2,3,0:T(8,128)S(1)} collective-permute-done((f32[3,34,16,1]{1,2,3,0:T(8,128)S(1)}, f32[3,34,16,1]{1,2,3,0:T(8,128)S(1)}, u32[]{:S(2)}, u32[]{:S(2)}) %collective-permute-start.27) | collective-permute-done | bytes 6560 | tf_op jit(solution)/shard_map/ppermute | solution.py:20
  162.5 3.3 %collective-permute-start.28 = (f32[3,1,16,128]{3,2,1,0:T(8,128)S(1)}, f32[3,1,16,128]{3,2,1,0:T(8,128)S(1)}, u32[]{:S(2)}, u32[]{:S(2)}) collective-permute-start(f32[3,1,16,128]{3,2,1,0:T(8,128)S(1)} %get-tuple-element.51), channel_id=1, source_target_pairs={{0,4},{4,8},{8,12},{12,16},{16,20},{20,24},{24,28},{1,5},{5,9},{9,... | collective-permute-start | bytes 73736 | tf_op jit(solution)/shard_map/ppermute | solution.py:19
  165.8 1.5 collective-permute-start.29
  167.3 4.2 %collective-permute-done.29 = f32[3,1,16,128]{3,2,1,0:T(8,128)S(1)} collective-permute-done((f32[3,1,16,128]{3,2,1,0:T(8,128)S(1)}, f32[3,1,16,128]{3,2,1,0:T(8,128)S(1)}, u32[]{:S(2)}, u32[]{:S(2)}) %collective-permute-start.29) | collective-permute-done | bytes 24608 | tf_op jit(solution)/shard_map/ppermute | solution.py:20
  172.3 3.5 %collective-permute-start.30 = (f32[3,34,16,1]{1,2,3,0:T(8,128)S(1)}, f32[3,34,16,1]{1,2,3,0:T(8,128)S(1)}, u32[]{:S(2)}, u32[]{:S(2)}) collective-permute-start(f32[3,34,16,1]{1,2,3,0:T(8,128)S(1)} %copy.106), channel_id=1, source_target_pairs={{0,1},{1,2},{2,3},{4,5},{5,6},{6,7},{8,9},{9,10},{10,11},{12,13},{... | collective-permute-start | bytes 19592 | tf_op jit(solution)/shard_map/ppermute | solution.py:19
  178.1 3.9 %collective-permute-done.31 = f32[3,34,16,1]{1,2,3,0:T(8,128)S(1)} collective-permute-done((f32[3,34,16,1]{1,2,3,0:T(8,128)S(1)}, f32[3,34,16,1]{1,2,3,0:T(8,128)S(1)}, u32[]{:S(2)}, u32[]{:S(2)}) %collective-permute-start.31) | collective-permute-done | bytes 6560 | tf_op jit(solution)/shard_map/ppermute | solution.py:20
  187.1 4.1 %collective-permute-start.32 = (f32[3,1,16,128]{3,2,1,0:T(8,128)S(1)}, f32[3,1,16,128]{3,2,1,0:T(8,128)S(1)}, u32[]{:S(2)}, u32[]{:S(2)}) collective-permute-start(f32[3,1,16,128]{3,2,1,0:T(8,128)S(1)} %get-tuple-element.49), channel_id=1, source_target_pairs={{0,4},{4,8},{8,12},{12,16},{16,20},{20,24},{24,28},{1,5},{5,9},{9,... | collective-permute-start | bytes 73736 | tf_op jit(solution)/shard_map/ppermute | solution.py:19
  192.7 4.4 %collective-permute-done.33 = f32[3,1,16,128]{3,2,1,0:T(8,128)S(1)} collective-permute-done((f32[3,1,16,128]{3,2,1,0:T(8,128)S(1)}, f32[3,1,16,128]{3,2,1,0:T(8,128)S(1)}, u32[]{:S(2)}, u32[]{:S(2)}) %collective-permute-start.33) | collective-permute-done | bytes 24608 | tf_op jit(solution)/shard_map/ppermute | solution.py:20
  197.9 2.2 collective-permute-start.34
  202.3 3.9 %collective-permute-done.35 = f32[3,34,16,1]{1,2,3,0:T(8,128)S(1)} collective-permute-done((f32[3,34,16,1]{1,2,3,0:T(8,128)S(1)}, f32[3,34,16,1]{1,2,3,0:T(8,128)S(1)}, u32[]{:S(2)}, u32[]{:S(2)}) %collective-permute-start.35) | collective-permute-done | bytes 6560 | tf_op jit(solution)/shard_map/ppermute | solution.py:20
  210.0 13.2 %all_to_all.27 = bf16[6,32,16,128]{3,1,0,2:T(8,128)(2,1)S(1)} all-to-all(bf16[6,32,16,128]{3,1,0,2:T(8,128)(2,1)S(1)} %copy.114), channel_id=1, replica_groups=mesh['gx'=4,'gy'=2,'gz'=4] {'gy'}, dimensions={2} | all-to-all | bytes 1572864 | tf_op jit(solution)/shard_map/all_to_all | solution.py:169
  223.2 1.4 copy.116
  (123 shorter events, 49.9 us)
Async XLA Ops:
  1.2 24.1 %copy-start.7 = (f32[64,8,128]{2,1,0:T(8,128)S(1)}, f32[64,8,128]{2,1,0:T(8,128)}, u32[]{:S(2)}) copy-start(f32[64,8,128]{2,1,0:T(8,128)} %param.5) | copy-start | bytes 786436
  2.4 3.7 %collective-permute-start = (bf16[3,1,8,128]{3,2,1,0:T(8,128)(2,1)S(1)}, bf16[3,1,8,128]{3,2,1,0:T(8,128)(2,1)S(1)}, u32[]{:S(2)}, u32[]{:S(2)}) collective-permute-start(bf16[3,1,8,128]{3,2,1,0:T(8,128)(2,1)S(1)} %get-tuple-element.66), channel_id=1, source_target_pairs={{0,8},{8,16},{16,24},{1,9},{9,17},{17,25},{2,10},{10,18},{18,26},{... | collective-permute-start | bytes 18440 | tf_op jit(solution)/shard_map/ppermute | solution.py:19
  4.8 5.2 %collective-permute-start.1 = (bf16[3,1,8,128]{3,2,1,0:T(8,128)(2,1)S(1)}, bf16[3,1,8,128]{3,2,1,0:T(8,128)(2,1)S(1)}, u32[]{:S(2)}, u32[]{:S(2)}) collective-permute-start(bf16[3,1,8,128]{3,2,1,0:T(8,128)(2,1)S(1)} %get-tuple-element.67), channel_id=1, source_target_pairs={{8,0},{16,8},{24,16},{9,1},{17,9},{25,17},{10,2},{18,10},{26,18},{... | collective-permute-start | bytes 18440 | tf_op jit(solution)/shard_map/ppermute | solution.py:20
  10.5 5.6 %collective-permute-start.2 = (bf16[3,66,1,128]{1,3,2,0:T(8,128)(2,1)S(1)}, bf16[3,66,1,128]{1,3,2,0:T(8,128)(2,1)S(1)}, u32[]{:S(2)}, u32[]{:S(2)}) collective-permute-start(bf16[3,66,1,128]{1,3,2,0:T(8,128)(2,1)S(1)} %get-tuple-element.55), channel_id=1, source_target_pairs={{0,4},{1,5},{2,6},{3,7},{8,12},{9,13},{10,14},{11,15},{16,20},{17,... | collective-permute-start | bytes 152072 | tf_op jit(solution)/shard_map/ppermute | solution.py:19
  14.0 6.5 %collective-permute-start.3 = (bf16[3,66,1,128]{1,3,2,0:T(8,128)(2,1)S(1)}, bf16[3,66,1,128]{1,3,2,0:T(8,128)(2,1)S(1)}, u32[]{:S(2)}, u32[]{:S(2)}) collective-permute-start(bf16[3,66,1,128]{1,3,2,0:T(8,128)(2,1)S(1)} %get-tuple-element.56), channel_id=1, source_target_pairs={{4,0},{5,1},{6,2},{7,3},{12,8},{13,9},{14,10},{15,11},{20,16},{21,... | collective-permute-start | bytes 152072 | tf_op jit(solution)/shard_map/ppermute | solution.py:20
  20.5 5.0 %collective-permute-start.4 = (bf16[3,66,10,1]{1,0,3,2:T(4,128)(2,1)S(1)}, bf16[3,66,10,1]{1,0,3,2:T(4,128)(2,1)S(1)}, u32[]{:S(2)}, u32[]{:S(2)}) collective-permute-start(bf16[3,66,10,1]{1,0,3,2:T(4,128)(2,1)S(1)} %copy.93), channel_id=1, source_target_pairs={{0,1},{1,2},{2,3},{4,5},{5,6},{6,7},{8,9},{9,10},{10,11},{12,13},{... | collective-permute-start | bytes 11888 | tf_op jit(solution)/shard_map/ppermute | solution.py:19
  24.0 5.6 %collective-permute-start.5 = (bf16[3,66,10,1]{1,0,3,2:T(4,128)(2,1)S(1)}, bf16[3,66,10,1]{1,0,3,2:T(4,128)(2,1)S(1)}, u32[]{:S(2)}, u32[]{:S(2)}) collective-permute-start(bf16[3,66,10,1]{1,0,3,2:T(4,128)(2,1)S(1)} %copy.94), channel_id=1, source_target_pairs={{1,0},{2,1},{3,2},{5,4},{6,5},{7,6},{9,8},{10,9},{11,10},{13,12},{... | collective-permute-start | bytes 11888 | tf_op jit(solution)/shard_map/ppermute | solution.py:20
  31.0 4.4 %collective-permute-start.6 = (f32[2,8,128]{0,2,1:T(8,128)S(1)}, f32[2,8,128]{0,2,1:T(8,128)S(1)}, u32[]{:S(2)}, u32[]{:S(2)}) collective-permute-start(f32[2,8,128]{0,2,1:T(8,128)S(1)} %get-tuple-element.65), channel_id=1, source_target_pairs={{8,0},{16,8},{24,16},{9,1},{17,9},{25,17},{10,2},{18,10},{26,18},{... | collective-permute-start | bytes 24584 | tf_op jit(solution)/shard_map/ppermute | solution.py:20
  32.3 4.6 %collective-permute-start.7 = (f32[2,8,128]{0,2,1:T(8,128)S(1)}, f32[2,8,128]{0,2,1:T(8,128)S(1)}, u32[]{:S(2)}, u32[]{:S(2)}) collective-permute-start(f32[2,8,128]{0,2,1:T(8,128)S(1)} %get-tuple-element.64), channel_id=1, source_target_pairs={{0,8},{8,16},{16,24},{1,9},{9,17},{17,25},{2,10},{10,18},{18,26},{... | collective-permute-start | bytes 24584 | tf_op jit(solution)/shard_map/ppermute | solution.py:19
  37.1 6.9 %collective-permute-start.8 = (f32[68,2,128]{0,2,1:T(8,128)S(1)}, f32[68,2,128]{0,2,1:T(8,128)S(1)}, u32[]{:S(2)}, u32[]{:S(2)}) collective-permute-start(f32[68,2,128]{0,2,1:T(8,128)S(1)} %get-tuple-element.40), channel_id=1, source_target_pairs={{4,0},{5,1},{6,2},{7,3},{12,8},{13,9},{14,10},{15,11},{20,16},{21,... | collective-permute-start | bytes 208904 | tf_op jit(solution)/shard_map/ppermute | solution.py:20
  38.4 7.1 %collective-permute-start.9 = (f32[68,2,128]{0,2,1:T(8,128)S(1)}, f32[68,2,128]{0,2,1:T(8,128)S(1)}, u32[]{:S(2)}, u32[]{:S(2)}) collective-permute-start(f32[68,2,128]{0,2,1:T(8,128)S(1)} %get-tuple-element.39), channel_id=1, source_target_pairs={{0,4},{1,5},{2,6},{3,7},{8,12},{9,13},{10,14},{11,15},{16,20},{17,... | collective-permute-start | bytes 208904 | tf_op jit(solution)/shard_map/ppermute | solution.py:19
  45.6 5.9 %collective-permute-start.10 = (f32[68,12,2]{0,2,1:T(2,128)S(1)}, f32[68,12,2]{0,2,1:T(2,128)S(1)}, u32[]{:S(2)}, u32[]{:S(2)}) collective-permute-start(f32[68,12,2]{0,2,1:T(2,128)S(1)} %get-tuple-element.33), channel_id=1, source_target_pairs={{1,0},{2,1},{3,2},{5,4},{6,5},{7,6},{9,8},{10,9},{11,10},{13,12},{... | collective-permute-start | bytes 19592 | tf_op jit(solution)/shard_map/ppermute | solution.py:20
  46.9 5.9 %collective-permute-start.11 = (f32[68,12,2]{0,2,1:T(2,128)S(1)}, f32[68,12,2]{0,2,1:T(2,128)S(1)}, u32[]{:S(2)}, u32[]{:S(2)}) collective-permute-start(f32[68,12,2]{0,2,1:T(2,128)S(1)} %get-tuple-element.34), channel_id=1, source_target_pairs={{0,1},{1,2},{2,3},{4,5},{5,6},{6,7},{8,9},{9,10},{10,11},{12,13},{... | collective-permute-start | bytes 19592 | tf_op jit(solution)/shard_map/ppermute | solution.py:19
  54.7 8.1 %collective-permute-start.12 = (f32[2,8,128]{0,2,1:T(8,128)S(1)}, f32[2,8,128]{0,2,1:T(8,128)S(1)}, u32[]{:S(2)}, u32[]{:S(2)}) collective-permute-start(f32[2,8,128]{0,2,1:T(8,128)S(1)} %get-tuple-element.63), channel_id=1, source_target_pairs={{8,0},{16,8},{24,16},{9,1},{17,9},{25,17},{10,2},{18,10},{26,18},{... | collective-permute-start | bytes 24584 | tf_op jit(solution)/shard_map/ppermute | solution.py:20
  56.0 8.3 %collective-permute-start.13 = (f32[2,8,128]{0,2,1:T(8,128)S(1)}, f32[2,8,128]{0,2,1:T(8,128)S(1)}, u32[]{:S(2)}, u32[]{:S(2)}) collective-permute-start(f32[2,8,128]{0,2,1:T(8,128)S(1)} %get-tuple-element.62), channel_id=1, source_target_pairs={{0,8},{8,16},{16,24},{1,9},{9,17},{17,25},{2,10},{10,18},{18,26},{... | collective-permute-start | bytes 24584 | tf_op jit(solution)/shard_map/ppermute | solution.py:19
  64.5 6.9 %collective-permute-start.14 = (f32[68,2,128]{0,2,1:T(8,128)S(1)}, f32[68,2,128]{0,2,1:T(8,128)S(1)}, u32[]{:S(2)}, u32[]{:S(2)}) collective-permute-start(f32[68,2,128]{0,2,1:T(8,128)S(1)} %get-tuple-element.38), channel_id=1, source_target_pairs={{4,0},{5,1},{6,2},{7,3},{12,8},{13,9},{14,10},{15,11},{20,16},{21,... | collective-permute-start | bytes 208904 | tf_op jit(solution)/shard_map/ppermute | solution.py:20
  65.8 7.1 %collective-permute-start.15 = (f32[68,2,128]{0,2,1:T(8,128)S(1)}, f32[68,2,128]{0,2,1:T(8,128)S(1)}, u32[]{:S(2)}, u32[]{:S(2)}) collective-permute-start(f32[68,2,128]{0,2,1:T(8,128)S(1)} %get-tuple-element.37), channel_id=1, source_target_pairs={{0,4},{1,5},{2,6},{3,7},{8,12},{9,13},{10,14},{11,15},{16,20},{17,... | collective-permute-start | bytes 208904 | tf_op jit(solution)/shard_map/ppermute | solution.py:19
  73.0 5.9 %collective-permute-start.16 = (f32[68,12,2]{0,2,1:T(2,128)S(1)}, f32[68,12,2]{0,2,1:T(2,128)S(1)}, u32[]{:S(2)}, u32[]{:S(2)}) collective-permute-start(f32[68,12,2]{0,2,1:T(2,128)S(1)} %get-tuple-element.31), channel_id=1, source_target_pairs={{1,0},{2,1},{3,2},{5,4},{6,5},{7,6},{9,8},{10,9},{11,10},{13,12},{... | collective-permute-start | bytes 19592 | tf_op jit(solution)/shard_map/ppermute | solution.py:20
  74.3 5.9 %collective-permute-start.17 = (f32[68,12,2]{0,2,1:T(2,128)S(1)}, f32[68,12,2]{0,2,1:T(2,128)S(1)}, u32[]{:S(2)}, u32[]{:S(2)}) collective-permute-start(f32[68,12,2]{0,2,1:T(2,128)S(1)} %get-tuple-element.32), channel_id=1, source_target_pairs={{0,1},{1,2},{2,3},{4,5},{5,6},{6,7},{8,9},{9,10},{10,11},{12,13},{... | collective-permute-start | bytes 19592 | tf_op jit(solution)/shard_map/ppermute | solution.py:19
  82.1 11.1 %collective-permute-start.18 = (f32[2,8,128]{0,2,1:T(8,128)S(1)}, f32[2,8,128]{0,2,1:T(8,128)S(1)}, u32[]{:S(2)}, u32[]{:S(2)}) collective-permute-start(f32[2,8,128]{0,2,1:T(8,128)S(1)} %get-tuple-element.60), channel_id=1, source_target_pairs={{0,8},{8,16},{16,24},{1,9},{9,17},{17,25},{2,10},{10,18},{18,26},{... | collective-permute-start | bytes 24584 | tf_op jit(solution)/shard_map/ppermute | solution.py:19
  91.8 7.7 %collective-permute-start.19 = (f32[2,8,128]{0,2,1:T(8,128)S(1)}, f32[2,8,128]{0,2,1:T(8,128)S(1)}, u32[]{:S(2)}, u32[]{:S(2)}) collective-permute-start(f32[2,8,128]{0,2,1:T(8,128)S(1)} %get-tuple-element.61), channel_id=1, source_target_pairs={{8,0},{16,8},{24,16},{9,1},{17,9},{25,17},{10,2},{18,10},{26,18},{... | collective-permute-start | bytes 24584 | tf_op jit(solution)/shard_map/ppermute | solution.py:20
  99.6 6.9 %collective-permute-start.20 = (f32[68,2,128]{0,2,1:T(8,128)S(1)}, f32[68,2,128]{0,2,1:T(8,128)S(1)}, u32[]{:S(2)}, u32[]{:S(2)}) collective-permute-start(f32[68,2,128]{0,2,1:T(8,128)S(1)} %get-tuple-element.35), channel_id=1, source_target_pairs={{0,4},{1,5},{2,6},{3,7},{8,12},{9,13},{10,14},{11,15},{16,20},{17,... | collective-permute-start | bytes 208904 | tf_op jit(solution)/shard_map/ppermute | solution.py:19
  104.0 6.9 %collective-permute-start.21 = (f32[68,2,128]{0,2,1:T(8,128)S(1)}, f32[68,2,128]{0,2,1:T(8,128)S(1)}, u32[]{:S(2)}, u32[]{:S(2)}) collective-permute-start(f32[68,2,128]{0,2,1:T(8,128)S(1)} %get-tuple-element.36), channel_id=1, source_target_pairs={{4,0},{5,1},{6,2},{7,3},{12,8},{13,9},{14,10},{15,11},{20,16},{21,... | collective-permute-start | bytes 208904 | tf_op jit(solution)/shard_map/ppermute | solution.py:20
  111.0 5.7 %collective-permute-start.22 = (f32[68,12,2]{0,2,1:T(2,128)S(1)}, f32[68,12,2]{0,2,1:T(2,128)S(1)}, u32[]{:S(2)}, u32[]{:S(2)}) collective-permute-start(f32[68,12,2]{0,2,1:T(2,128)S(1)} %get-tuple-element.29), channel_id=1, source_target_pairs={{0,1},{1,2},{2,3},{4,5},{5,6},{6,7},{8,9},{9,10},{10,11},{12,13},{... | collective-permute-start | bytes 19592 | tf_op jit(solution)/shard_map/ppermute | solution.py:19
  115.2 5.6 %collective-permute-start.23 = (f32[68,12,2]{0,2,1:T(2,128)S(1)}, f32[68,12,2]{0,2,1:T(2,128)S(1)}, u32[]{:S(2)}, u32[]{:S(2)}) collective-permute-start(f32[68,12,2]{0,2,1:T(2,128)S(1)} %get-tuple-element.30), channel_id=1, source_target_pairs={{1,0},{2,1},{3,2},{5,4},{6,5},{7,6},{9,8},{10,9},{11,10},{13,12},{... | collective-permute-start | bytes 19592 | tf_op jit(solution)/shard_map/ppermute | solution.py:20
  125.4 4.7 %copy-start.4 = (f32[32,16,128]{2,1,0:T(8,128)S(1)}, f32[32,16,128]{2,1,0:T(8,128)}, u32[]{:S(2)}) copy-start(f32[32,16,128]{2,1,0:T(8,128)} %param.7) | copy-start | bytes 786436
  126.6 9.3 %all-to-all-start = ((bf16[3,64,8,128]{3,2,0,1:T(8,128)(2,1)}), bf16[3,64,8,128]{3,2,0,1:T(8,128)(2,1)S(1)}, u32[]{:S(2)}, u32[]{:S(2)}) async-start(bf16[3,64,8,128]{3,2,0,1:T(8,128)(2,1)} %copy.99), calls=%async_computation | async-start | bytes 786432 | tf_op jit(solution)/shard_map/all_to_all | solution.py:161
  136.2 3.4 %collective-permute-start.24 = (f32[3,1,16,128]{3,2,1,0:T(8,128)S(1)}, f32[3,1,16,128]{3,2,1,0:T(8,128)S(1)}, u32[]{:S(2)}, u32[]{:S(2)}) collective-permute-start(f32[3,1,16,128]{3,2,1,0:T(8,128)S(1)} %get-tuple-element.53), channel_id=1, source_target_pairs={{0,4},{4,8},{8,12},{12,16},{16,20},{20,24},{24,28},{1,5},{5,9},{9,... | collective-permute-start | bytes 73736 | tf_op jit(solution)/shard_map/ppermute | solution.py:19
  138.1 8.8 %collective-permute-start.25 = (f32[3,1,16,128]{3,2,1,0:T(8,128)S(1)}, f32[3,1,16,128]{3,2,1,0:T(8,128)S(1)}, u32[]{:S(2)}, u32[]{:S(2)}) collective-permute-start(f32[3,1,16,128]{3,2,1,0:T(8,128)S(1)} %get-tuple-element.54), channel_id=1, source_target_pairs={{4,0},{8,4},{12,8},{16,12},{20,16},{24,20},{28,24},{5,1},{9,5},{13... | collective-permute-start | bytes 73736 | tf_op jit(solution)/shard_map/ppermute | solution.py:20
  147.7 5.4 %collective-permute-start.26 = (f32[3,34,16,1]{1,2,3,0:T(8,128)S(1)}, f32[3,34,16,1]{1,2,3,0:T(8,128)S(1)}, u32[]{:S(2)}, u32[]{:S(2)}) collective-permute-start(f32[3,34,16,1]{1,2,3,0:T(8,128)S(1)} %copy.102), channel_id=1, source_target_pairs={{0,1},{1,2},{2,3},{4,5},{5,6},{6,7},{8,9},{9,10},{10,11},{12,13},{... | collective-permute-start | bytes 19592 | tf_op jit(solution)/shard_map/ppermute | solution.py:19
  151.8 5.7 %collective-permute-start.27 = (f32[3,34,16,1]{1,2,3,0:T(8,128)S(1)}, f32[3,34,16,1]{1,2,3,0:T(8,128)S(1)}, u32[]{:S(2)}, u32[]{:S(2)}) collective-permute-start(f32[3,34,16,1]{1,2,3,0:T(8,128)S(1)} %copy.103), channel_id=1, source_target_pairs={{1,0},{2,1},{3,2},{5,4},{6,5},{7,6},{9,8},{10,9},{11,10},{13,12},{... | collective-permute-start | bytes 19592 | tf_op jit(solution)/shard_map/ppermute | solution.py:20
  161.2 1.3 copy-start
  161.2 1.0 copy-start.5
  162.2 9.3 %copy-start.2 = (f32[1,32,16,128]{3,2,1,0:T(8,128)}, f32[1,32,16,128]{3,2,1,0:T(8,128)S(1)}, u32[]{:S(2)}) copy-start(f32[1,32,16,128]{3,2,1,0:T(8,128)S(1)} %fusion.100) | copy-start | bytes 786436
  162.5 4.9 %collective-permute-start.28 = (f32[3,1,16,128]{3,2,1,0:T(8,128)S(1)}, f32[3,1,16,128]{3,2,1,0:T(8,128)S(1)}, u32[]{:S(2)}, u32[]{:S(2)}) collective-permute-start(f32[3,1,16,128]{3,2,1,0:T(8,128)S(1)} %get-tuple-element.51), channel_id=1, source_target_pairs={{0,4},{4,8},{8,12},{12,16},{16,20},{20,24},{24,28},{1,5},{5,9},{9,... | collective-permute-start | bytes 73736 | tf_op jit(solution)/shard_map/ppermute | solution.py:19
  165.8 5.7 %collective-permute-start.29 = (f32[3,1,16,128]{3,2,1,0:T(8,128)S(1)}, f32[3,1,16,128]{3,2,1,0:T(8,128)S(1)}, u32[]{:S(2)}, u32[]{:S(2)}) collective-permute-start(f32[3,1,16,128]{3,2,1,0:T(8,128)S(1)} %get-tuple-element.52), channel_id=1, source_target_pairs={{4,0},{8,4},{12,8},{16,12},{20,16},{24,20},{28,24},{5,1},{9,5},{13... | collective-permute-start | bytes 73736 | tf_op jit(solution)/shard_map/ppermute | solution.py:20
  172.3 5.2 %collective-permute-start.30 = (f32[3,34,16,1]{1,2,3,0:T(8,128)S(1)}, f32[3,34,16,1]{1,2,3,0:T(8,128)S(1)}, u32[]{:S(2)}, u32[]{:S(2)}) collective-permute-start(f32[3,34,16,1]{1,2,3,0:T(8,128)S(1)} %copy.106), channel_id=1, source_target_pairs={{0,1},{1,2},{2,3},{4,5},{5,6},{6,7},{8,9},{9,10},{10,11},{12,13},{... | collective-permute-start | bytes 19592 | tf_op jit(solution)/shard_map/ppermute | solution.py:19
  176.3 5.7 %collective-permute-start.31 = (f32[3,34,16,1]{1,2,3,0:T(8,128)S(1)}, f32[3,34,16,1]{1,2,3,0:T(8,128)S(1)}, u32[]{:S(2)}, u32[]{:S(2)}) collective-permute-start(f32[3,34,16,1]{1,2,3,0:T(8,128)S(1)} %copy.107), channel_id=1, source_target_pairs={{1,0},{2,1},{3,2},{5,4},{6,5},{7,6},{9,8},{10,9},{11,10},{13,12},{... | collective-permute-start | bytes 19592 | tf_op jit(solution)/shard_map/ppermute | solution.py:20
  185.6 1.0 copy-start.1
  185.6 1.0 copy-start.3
  185.6 1.1 copy-start.6
  187.1 5.6 %collective-permute-start.32 = (f32[3,1,16,128]{3,2,1,0:T(8,128)S(1)}, f32[3,1,16,128]{3,2,1,0:T(8,128)S(1)}, u32[]{:S(2)}, u32[]{:S(2)}) collective-permute-start(f32[3,1,16,128]{3,2,1,0:T(8,128)S(1)} %get-tuple-element.49), channel_id=1, source_target_pairs={{0,4},{4,8},{8,12},{12,16},{16,20},{20,24},{24,28},{1,5},{5,9},{9,... | collective-permute-start | bytes 73736 | tf_op jit(solution)/shard_map/ppermute | solution.py:19
  191.2 5.9 %collective-permute-start.33 = (f32[3,1,16,128]{3,2,1,0:T(8,128)S(1)}, f32[3,1,16,128]{3,2,1,0:T(8,128)S(1)}, u32[]{:S(2)}, u32[]{:S(2)}) collective-permute-start(f32[3,1,16,128]{3,2,1,0:T(8,128)S(1)} %get-tuple-element.50), channel_id=1, source_target_pairs={{4,0},{8,4},{12,8},{16,12},{20,16},{24,20},{28,24},{5,1},{9,5},{13... | collective-permute-start | bytes 73736 | tf_op jit(solution)/shard_map/ppermute | solution.py:20
  197.9 3.9 %collective-permute-start.34 = (f32[3,34,16,1]{1,2,3,0:T(8,128)S(1)}, f32[3,34,16,1]{1,2,3,0:T(8,128)S(1)}, u32[]{:S(2)}, u32[]{:S(2)}) collective-permute-start(f32[3,34,16,1]{1,2,3,0:T(8,128)S(1)} %copy.110), channel_id=1, source_target_pairs={{0,1},{1,2},{2,3},{4,5},{5,6},{6,7},{8,9},{9,10},{10,11},{12,13},{... | collective-permute-start | bytes 19592 | tf_op jit(solution)/shard_map/ppermute | solution.py:19
  200.5 5.7 %collective-permute-start.35 = (f32[3,34,16,1]{1,2,3,0:T(8,128)S(1)}, f32[3,34,16,1]{1,2,3,0:T(8,128)S(1)}, u32[]{:S(2)}, u32[]{:S(2)}) collective-permute-start(f32[3,34,16,1]{1,2,3,0:T(8,128)S(1)} %copy.111), channel_id=1, source_target_pairs={{1,0},{2,1},{3,2},{5,4},{6,5},{7,6},{9,8},{10,9},{11,10},{13,12},{... | collective-permute-start | bytes 19592 | tf_op jit(solution)/shard_map/ppermute | solution.py:20
where the time goes:
time: 226 us; the launch traced here: 225 us
  starting transfers between devices  101 us (45%)
  waiting for transfers between devices  73.7 us (33%)
  other arithmetic  22.4 us (10%)
  local copies, waits for them, and re-layouts  13.2 us (6%)
  blocking collectives  13.2 us (6%)
    ppermute x18, starting transfers between devices, padded_2(): before = lax.ppermute(last, axis, up)  74.2 us
    ppermute x18, waiting for transfers between devices, padded_2(): after = lax.ppermute(leading, axis, down)  56.5 us
    ppermute x18, starting transfers between devices, padded_2(): after = lax.ppermute(leading, axis, down)  23.6 us
    all_to_all x1, blocking collectives, per_device(): return lax.all_to_all(strain, 'gy', split_axis=2, concat_axis=1, tiled=True)  13.2 us
    ppermute x18, waiting for transfers between devices, padded_2(): before = lax.ppermute(last, axis, up)  11.4 us
    all_to_all x1, waiting for transfers between devices, per_device(): lax.all_to_all(force, 'gy', split_axis=1, concat_axis=2, tiled=True)  5.82 us
    another operation x6, other arithmetic, navier(): return jnp.stack(result)  5.01 us
    concatenate x10, other arithmetic, padded_2(): value = jnp.concatenate([before, value, after], axis=dim)  4.53 us
  transfers between devices with their start and end apart: 37, of which 26 were waited for; matrix products, arithmetic and copies ran while one was open for 1% of the time, Pallas kernels for 0%

commit v1 on v0

--- a/solution.py
+++ b/solution.py
@@ -3,10 +3,23 @@
 import jax.numpy as jnp
 from jax import lax
 from jax.sharding import PartitionSpec as P
+from jax.lax import all_to_all, axis_size
 
 SWEEPS = 3
 STRAIN_PAIRS = ((0, 0), (1, 1), (2, 2), (0, 1), (1, 2), (0, 2))
 MAGNETO = 4.0
+
+
+def point_column(axis_k, dim_k, inner_x):
+    return jnp.concatenate(
+        all_to_all(
+            jnp.stack(jnp.split(inner_x, axis_size("gy"), dim_k), axis=0),
+            concat_axis=0,
+            axis_name="gy",
+            split_axis=0,
+        ),
+        axis_k,
+    )
 
 
 def padded_2(value, sides, width):
@@ -166,7 +179,7 @@
 
     displacement = elastic_solve(load, stiffness, pad_slab)
     strain = strain_from(pad_slab(displacement)).astype(jnp.bfloat16)
-    return lax.all_to_all(strain, "gy", split_axis=2, concat_axis=1, tiled=True)
+    return point_column(1, dim_k=2, inner_x=strain)
 
 
 def solution(mesh):

time: 226 us -> 237 us (1.049)
  local copies, waits for them, and re-layouts: 13.2 us -> 38.7 us
  starting transfers between devices: 101 us -> 89.4 us
  waiting for transfers between devices: 73.7 us -> 62.6 us
  other arithmetic: 22.4 us -> 30.5 us
    ppermute x18, starting transfers between devices: 74.2 us -> 62.4 us  [padded_2(): before = lax.ppermute(last, axis, up)]
    ppermute x18, waiting for transfers between devices: 56.5 us -> 48.9 us  [padded_2(): after = lax.ppermute(leading, axis, down)]
    slice x4 -> x7, local copies, waits for them, and re-layouts: 1.36 us -> 7.52 us  [padded_2(): leading = lax.slice_in_dim(value, 0, width, axis=dim)]
    ppermute x4 -> x8, local copies, waits for them, and re-layouts: 1.51 us -> 7.23 us  [padded_2(): after = lax.ppermute(leading, axis, down)]
    ppermute x4 -> x8, local copies, waits for them, and re-layouts: 1.51 us -> 7.17 us  [padded_2(): before = lax.ppermute(last, axis, up)]
    ppermute x18, waiting for transfers between devices: 11.4 us -> 6.56 us  [padded_2(): before = lax.ppermute(last, axis, up)]
    slice x15 -> x17, local copies, waits for them, and re-layouts: 2.88 us -> 7.61 us  [padded_2(): last = lax.slice_in_dim(value, length - width, length, axis=dim)]
    unnamed x18 -> x48, local copies, waits for them, and re-layouts: 2 us -> 6.43 us
  transfers between devices with their start and end apart: 37 -> 37, of which waited for: 26 -> 24; matrix products, arithmetic and copies ran while one was open for 1% -> 6% of each run, Pallas kernels for 0% -> 0%
where the time goes in v1:
time: 237 us; the launch traced here: 235 us
  starting transfers between devices  89.4 us (38%)
  waiting for transfers between devices  62.6 us (26%)
  local copies, waits for them, and re-layouts  38.7 us (16%)
  other arithmetic  30.5 us (13%)
  blocking collectives  13.2 us (6%)
    ppermute x18, starting transfers between devices, padded_2(): before = lax.ppermute(last, axis, up)  62.4 us
    ppermute x18, waiting for transfers between devices, padded_2(): after = lax.ppermute(leading, axis, down)  48.9 us
    ppermute x18, starting transfers between devices, padded_2(): after = lax.ppermute(leading, axis, down)  23.6 us
    all_to_all x1, blocking collectives, point_column(): all_to_all(jnp.stack(jnp.split(inner_x, axis_size('gy'), dim_k), axis=0),...  13.2 us
    slice x17, local copies, waits for them, and re-layouts, padded_2(): last = lax.slice_in_dim(value, length - width, length, axis=dim)  7.61 us
    slice x7, local copies, waits for them, and re-layouts, padded_2(): leading = lax.slice_in_dim(value, 0, width, axis=dim)  7.52 us
    ppermute x8, local copies, waits for them, and re-layouts, padded_2(): after = lax.ppermute(leading, axis, down)  7.23 us
    ppermute x8, local copies, waits for them, and re-layouts, padded_2(): before = lax.ppermute(last, axis, up)  7.17 us
  transfers between devices with their start and end apart: 37, of which 24 were waited for; matrix products, arithmetic and copies ran while one was open for 6% of the time, Pallas kernels for 0%

profile of v1, /device:TPU:0, one launch (start us, length us, event | category | flops | bytes accessed | tf_op | source)
XLA Modules:
  0.0 235.3 jit_solution(17034764095796212313)
XLA Ops:
  2.0 2.4 %collective-permute-start = (bf16[3,1,8,128]{3,2,1,0:T(8,128)(2,1)S(1)}, bf16[3,1,8,128]{3,2,1,0:T(8,128)(2,1)S(1)}, u32[]{:S(2)}, u32[]{:S(2)}) collective-permute-start(bf16[3,1,8,128]{3,2,1,0:T(8,128)(2,1)S(1)} %get-tuple-element.56), channel_id=1, source_target_pairs={{0,8},{8,16},{16,24},{1,9},{9,17},{17,25},{2,10},{10,18},{18,26},{... | collective-permute-start | bytes 18440 | tf_op jit(solution)/shard_map/ppermute | solution.py:32
  5.7 3.9 %collective-permute-done.1 = bf16[3,1,8,128]{3,2,1,0:T(8,128)(2,1)S(1)} collective-permute-done((bf16[3,1,8,128]{3,2,1,0:T(8,128)(2,1)S(1)}, bf16[3,1,8,128]{3,2,1,0:T(8,128)(2,1)S(1)}, u32[]{:S(2)}, u32[]{:S(2)}) %collective-permute-start.1) | collective-permute-done | bytes 6176 | tf_op jit(solution)/shard_map/ppermute | solution.py:33
  9.7 3.4 %collective-permute-start.2 = (bf16[3,66,1,128]{3,1,2,0:T(8,128)(2,1)S(1)}, bf16[3,66,1,128]{3,1,2,0:T(8,128)(2,1)S(1)}, u32[]{:S(2)}, u32[]{:S(2)}) collective-permute-start(bf16[3,66,1,128]{3,1,2,0:T(8,128)(2,1)S(1)} %copy.120), channel_id=1, source_target_pairs={{0,4},{1,5},{2,6},{3,7},{8,12},{9,13},{10,14},{11,15},{16,20},{17,... | collective-permute-start | bytes 152072 | tf_op jit(solution)/shard_map/ppermute | solution.py:32
  15.0 4.2 %collective-permute-done.3 = bf16[3,66,1,128]{3,1,2,0:T(8,128)(2,1)S(1)} collective-permute-done((bf16[3,66,1,128]{3,1,2,0:T(8,128)(2,1)S(1)}, bf16[3,66,1,128]{3,1,2,0:T(8,128)(2,1)S(1)}, u32[]{:S(2)}, u32[]{:S(2)}) %collective-permute-start.3) | collective-permute-done | bytes 50720 | tf_op jit(solution)/shard_map/ppermute | solution.py:33
  21.0 3.5 %collective-permute-start.4 = (bf16[3,66,10,1]{1,2,3,0:T(8,128)(2,1)S(1)}, bf16[3,66,10,1]{1,2,3,0:T(8,128)(2,1)S(1)}, u32[]{:S(2)}, u32[]{:S(2)}) collective-permute-start(bf16[3,66,10,1]{1,2,3,0:T(8,128)(2,1)S(1)} %copy.124), channel_id=1, source_target_pairs={{0,1},{1,2},{2,3},{4,5},{5,6},{6,7},{8,9},{9,10},{10,11},{12,13},{... | collective-permute-start | bytes 11888 | tf_op jit(solution)/shard_map/ppermute | solution.py:32
  26.5 1.6 copy.126
  28.1 2.7 %collective-permute-done.5 = bf16[3,66,10,1]{1,2,3,0:T(8,128)(2,1)S(1)} collective-permute-done((bf16[3,66,10,1]{1,2,3,0:T(8,128)(2,1)S(1)}, bf16[3,66,10,1]{1,2,3,0:T(8,128)(2,1)S(1)}, u32[]{:S(2)}, u32[]{:S(2)}) %collective-permute-start.5) | collective-permute-done | bytes 3992 | tf_op jit(solution)/shard_map/ppermute | solution.py:33
  30.8 1.6 copy.127
  32.4 3.2 %maximum_convert_fusion = f32[3,66,10,130]{3,2,1,0:T(8,128)S(1)} fusion(bf16[3,66,10,1]{3,2,1,0:T(8,128)(2,1)} %copy.127, bf16[3,66,1,128]{3,2,1,0:T(2,128)(2,1)S(1)} %copy.123, bf16[3,1,8,128]{3,2,1,0:T(8,128)(2,1)S(1)} %collective-permute-done.1, bf16[3,64,8,128]{3,2,1,0:T(8,128)(2,1)} %copy-done, bf16[3,1,8,128]{3,2,1,0:T(8,128)(2,1)S(1)} %collective-permute-done, ...), kind=kLoop, calls=%fused_computation.15 | loop fusion | flops 3603600 | bytes 1544400 | tf_op jit(solution)/shard_map/convert_element_type | solution.py:160
  39.0 3.0 %collective-permute-start.7 = (f32[2,8,128]{2,1,0:T(8,128)S(1)}, f32[2,8,128]{2,1,0:T(8,128)S(1)}, u32[]{:S(2)}, u32[]{:S(2)}) collective-permute-start(f32[2,8,128]{2,1,0:T(8,128)S(1)} %get-tuple-element.68), channel_id=1, source_target_pairs={{0,8},{8,16},{16,24},{1,9},{9,17},{17,25},{2,10},{10,18},{18,26},{... | collective-permute-start | bytes 24584 | tf_op jit(solution)/shard_map/ppermute | solution.py:32
  44.2 4.5 %collective-permute-start.9 = (f32[68,2,128]{2,1,0:T(2,128)S(1)}, f32[68,2,128]{2,1,0:T(2,128)S(1)}, u32[]{:S(2)}, u32[]{:S(2)}) collective-permute-start(f32[68,2,128]{2,1,0:T(2,128)S(1)} %get-tuple-element.62), channel_id=1, source_target_pairs={{0,4},{1,5},{2,6},{3,7},{8,12},{9,13},{10,14},{11,15},{16,20},{17,... | collective-permute-start | bytes 208904 | tf_op jit(solution)/shard_map/ppermute | solution.py:32
  49.1 1.6 collective-permute-done.9
  55.2 1.9 copy.130
  57.1 5.1 %collective-permute-start.11 = (f32[68,12,2]{0,2,1:T(2,128)}, f32[68,12,2]{0,2,1:T(2,128)}, u32[]{:S(2)}, u32[]{:S(2)}) collective-permute-start(f32[68,12,2]{0,2,1:T(2,128)} %copy.130), channel_id=1, source_target_pairs={{0,1},{1,2},{2,3},{4,5},{5,6},{6,7},{8,9},{9,10},{10,11},{12,13},{... | collective-permute-start | bytes 19592 | tf_op jit(solution)/shard_map/ppermute | solution.py:32
  63.3 1.8 copy.131
  65.1 2.0 fusion.113
  68.5 3.0 %collective-permute-start.13 = (f32[2,8,128]{2,1,0:T(8,128)S(1)}, f32[2,8,128]{2,1,0:T(8,128)S(1)}, u32[]{:S(2)}, u32[]{:S(2)}) collective-permute-start(f32[2,8,128]{2,1,0:T(8,128)S(1)} %get-tuple-element.66), channel_id=1, source_target_pairs={{0,8},{8,16},{16,24},{1,9},{9,17},{17,25},{2,10},{10,18},{18,26},{... | collective-permute-start | bytes 24584 | tf_op jit(solution)/shard_map/ppermute | solution.py:32
  73.7 4.5 %collective-permute-start.15 = (f32[68,2,128]{2,1,0:T(2,128)S(1)}, f32[68,2,128]{2,1,0:T(2,128)S(1)}, u32[]{:S(2)}, u32[]{:S(2)}) collective-permute-start(f32[68,2,128]{2,1,0:T(2,128)S(1)} %get-tuple-element.60), channel_id=1, source_target_pairs={{0,4},{1,5},{2,6},{3,7},{8,12},{9,13},{10,14},{11,15},{16,20},{17,... | collective-permute-start | bytes 208904 | tf_op jit(solution)/shard_map/ppermute | solution.py:32
  78.6 1.6 collective-permute-done.15
  85.9 4.8 %collective-permute-start.17 = (f32[68,12,2]{0,2,1:T(2,128)S(1)}, f32[68,12,2]{0,2,1:T(2,128)S(1)}, u32[]{:S(2)}, u32[]{:S(2)}) collective-permute-start(f32[68,12,2]{0,2,1:T(2,128)S(1)} %copy.134), channel_id=1, source_target_pairs={{0,1},{1,2},{2,3},{4,5},{5,6},{6,7},{8,9},{9,10},{10,11},{12,13},{... | collective-permute-start | bytes 19592 | tf_op jit(solution)/shard_map/ppermute | solution.py:32
  93.2 2.7 %fusion.103 = f32[64,8,128]{2,1,0:T(8,128)S(1)} fusion(f32[64,8,128]{2,1,0:T(8,128)} %copy-done.3, f32[64,8,128]{2,1,0:T(8,128)} %get-tuple-element.11, f32[68,12,2]{2,1,0:T(8,128)} %copy.135, f32[68,2,128]{2,1,0:T(2,128)} %copy-done.18, f32[68,2,128]{2,1,0:T(2,128)} %copy-done.20, f32[2,8,128]{2,1,0:T(8,128)S(1)} %collective-permute-done.12, ...), kind=kLoop, calls=%fused_computation.240 | loop fusion | flops 2359296 | bytes 1479424 | tf_op jit(solution)/shard_map/add | solution.py:168
  95.9 3.8 %collective-permute-start.18 = (f32[2,8,128]{2,1,0:T(8,128)S(1)}, f32[2,8,128]{2,1,0:T(8,128)S(1)}, u32[]{:S(2)}, u32[]{:S(2)}) collective-permute-start(f32[2,8,128]{2,1,0:T(8,128)S(1)} %get-tuple-element.64), channel_id=1, source_target_pairs={{0,8},{8,16},{16,24},{1,9},{9,17},{17,25},{2,10},{10,18},{18,26},{... | collective-permute-start | bytes 24584 | tf_op jit(solution)/shard_map/ppermute | solution.py:32
  101.1 5.2 %collective-permute-done.19 = f32[2,8,128]{2,1,0:T(8,128)S(1)} collective-permute-done((f32[2,8,128]{2,1,0:T(8,128)S(1)}, f32[2,8,128]{2,1,0:T(8,128)S(1)}, u32[]{:S(2)}, u32[]{:S(2)}) %collective-permute-start.19) | collective-permute-done | bytes 8224 | tf_op jit(solution)/shard_map/ppermute | solution.py:33
  106.3 4.3 %collective-permute-start.20 = (f32[68,2,128]{2,1,0:T(2,128)S(1)}, f32[68,2,128]{2,1,0:T(2,128)S(1)}, u32[]{:S(2)}, u32[]{:S(2)}) collective-permute-start(f32[68,2,128]{2,1,0:T(2,128)S(1)} %get-tuple-element.58), channel_id=1, source_target_pairs={{0,4},{1,5},{2,6},{3,7},{8,12},{9,13},{10,14},{11,15},{16,20},{17,... | collective-permute-start | bytes 208904 | tf_op jit(solution)/shard_map/ppermute | solution.py:32
  112.5 4.3 %collective-permute-done.21 = f32[68,2,128]{2,1,0:T(2,128)S(1)} collective-permute-done((f32[68,2,128]{2,1,0:T(2,128)S(1)}, f32[68,2,128]{2,1,0:T(2,128)S(1)}, u32[]{:S(2)}, u32[]{:S(2)}) %collective-permute-start.21) | collective-permute-done | bytes 69664 | tf_op jit(solution)/shard_map/ppermute | solution.py:33
  120.0 4.2 %collective-permute-start.22 = (f32[68,12,2]{0,2,1:T(2,128)S(1)}, f32[68,12,2]{0,2,1:T(2,128)S(1)}, u32[]{:S(2)}, u32[]{:S(2)}) collective-permute-start(f32[68,12,2]{0,2,1:T(2,128)S(1)} %copy.136), channel_id=1, source_target_pairs={{0,1},{1,2},{2,3},{4,5},{5,6},{6,7},{8,9},{9,10},{10,11},{12,13},{... | collective-permute-start | bytes 19592 | tf_op jit(solution)/shard_map/ppermute | solution.py:32
  124.2 1.9 copy.137
  126.0 1.5 collective-permute-start.23
  128.6 3.4 %collective-permute-done.23 = f32[68,12,2]{0,2,1:T(2,128)} collective-permute-done((f32[68,12,2]{0,2,1:T(2,128)}, f32[68,12,2]{0,2,1:T(2,128)}, u32[]{:S(2)}, u32[]{:S(2)}) %collective-permute-start.23) | collective-permute-done | bytes 6560 | tf_op jit(solution)/shard_map/ppermute | solution.py:33
  132.1 1.8 copy.139
  133.9 2.2 pad_maximum_fusion
  136.1 3.0 %subtract_multiply_fusion.2 = (f32[66,10,130]{2,1,0:T(8,128)S(1)}, f32[66,10,130]{2,1,0:T(8,128)S(1)}, f32[66,10,130]{2,1,0:T(8,128)S(1)}, f32[66,10,130]{2,1,0:T(8,128)S(1)}, f32[66,10,130]{2,1,0:T(8,128)S(1)}) fusion(f32[3,66,10,130]{3,2,1,0:T(8,128)S(1)} %maximum_convert_fusion, f32[68,12,132]{2,1,0:T(8,128)S(1)} %pad_maximum_fusion, ...), kind=kLoop, calls=%fused_computation.44 | loop fusion | flops 2488200 | bytes 4549248 | tf_op jit(solution)/shard_map/mul | solution.py:85
  142.0 3.5 %all-to-all-start = ((bf16[3,64,8,128]{3,2,0,1:T(8,128)(2,1)}), bf16[3,64,8,128]{3,2,0,1:T(8,128)(2,1)S(1)}, u32[]{:S(2)}, u32[]{:S(2)}) async-start(bf16[3,64,8,128]{3,2,0,1:T(8,128)(2,1)} %copy.142), calls=%async_computation | async-start | bytes 786432 | tf_op jit(solution)/shard_map/all_to_all | solution.py:174
  145.5 7.1 %all-to-all-done = bf16[3,64,8,128]{3,2,0,1:T(8,128)(2,1)S(1)} async-done(((bf16[3,64,8,128]{3,2,0,1:T(8,128)(2,1)}), bf16[3,64,8,128]{3,2,0,1:T(8,128)(2,1)S(1)}, u32[]{:S(2)}, u32[]{:S(2)}) %all-to-all-start) | async-done | bytes 393248 | tf_op jit(solution)/shard_map/all_to_all | solution.py:174
  152.7 2.2 collective-permute-start.24
  156.4 4.2 %collective-permute-done.25 = f32[3,1,16,128]{3,2,1,0:T(8,128)S(1)} collective-permute-done((f32[3,1,16,128]{3,2,1,0:T(8,128)S(1)}, f32[3,1,16,128]{3,2,1,0:T(8,128)S(1)}, u32[]{:S(2)}, u32[]{:S(2)}) %collective-permute-start.25) | collective-permute-done | bytes 24608 | tf_op jit(solution)/shard_map/ppermute | solution.py:33
  161.5 3.2 %collective-permute-start.26 = (f32[3,34,16,1]{1,2,3,0:T(8,128)S(1)}, f32[3,34,16,1]{1,2,3,0:T(8,128)S(1)}, u32[]{:S(2)}, u32[]{:S(2)}) collective-permute-start(f32[3,34,16,1]{1,2,3,0:T(8,128)S(1)} %copy.157), channel_id=1, source_target_pairs={{0,1},{1,2},{2,3},{4,5},{5,6},{6,7},{8,9},{9,10},{10,11},{12,13},{... | collective-permute-start | bytes 19592 | tf_op jit(solution)/shard_map/ppermute | solution.py:32
  167.0 3.9 %collective-permute-done.27 = f32[3,34,16,1]{1,2,3,0:T(8,128)S(1)} collective-permute-done((f32[3,34,16,1]{1,2,3,0:T(8,128)S(1)}, f32[3,34,16,1]{1,2,3,0:T(8,128)S(1)}, u32[]{:S(2)}, u32[]{:S(2)}) %collective-permute-start.27) | collective-permute-done | bytes 6560 | tf_op jit(solution)/shard_map/ppermute | solution.py:33
  176.3 1.6 collective-permute-start.28
  177.9 1.5 collective-permute-start.29
  179.4 4.2 %collective-permute-done.29 = f32[3,1,16,128]{3,2,1,0:T(8,128)S(1)} collective-permute-done((f32[3,1,16,128]{3,2,1,0:T(8,128)S(1)}, f32[3,1,16,128]{3,2,1,0:T(8,128)S(1)}, u32[]{:S(2)}, u32[]{:S(2)}) %collective-permute-start.29) | collective-permute-done | bytes 24608 | tf_op jit(solution)/shard_map/ppermute | solution.py:33
  184.4 3.5 %collective-permute-start.30 = (f32[3,34,16,1]{1,2,3,0:T(8,128)S(1)}, f32[3,34,16,1]{1,2,3,0:T(8,128)S(1)}, u32[]{:S(2)}, u32[]{:S(2)}) collective-permute-start(f32[3,34,16,1]{1,2,3,0:T(8,128)S(1)} %copy.159), channel_id=1, source_target_pairs={{0,1},{1,2},{2,3},{4,5},{5,6},{6,7},{8,9},{9,10},{10,11},{12,13},{... | collective-permute-start | bytes 19592 | tf_op jit(solution)/shard_map/ppermute | solution.py:32
  190.1 3.9 %collective-permute-done.31 = f32[3,34,16,1]{1,2,3,0:T(8,128)S(1)} collective-permute-done((f32[3,34,16,1]{1,2,3,0:T(8,128)S(1)}, f32[3,34,16,1]{1,2,3,0:T(8,128)S(1)}, u32[]{:S(2)}, u32[]{:S(2)}) %collective-permute-start.31) | collective-permute-done | bytes 6560 | tf_op jit(solution)/shard_map/ppermute | solution.py:33
  199.1 3.1 %collective-permute-start.32 = (f32[3,1,16,128]{3,2,1,0:T(8,128)S(1)}, f32[3,1,16,128]{3,2,1,0:T(8,128)S(1)}, u32[]{:S(2)}, u32[]{:S(2)}) collective-permute-start(f32[3,1,16,128]{3,2,1,0:T(8,128)S(1)} %get-tuple-element.42), channel_id=1, source_target_pairs={{0,4},{4,8},{8,12},{12,16},{16,20},{20,24},{24,28},{1,5},{5,9},{9,... | collective-permute-start | bytes 73736 | tf_op jit(solution)/shard_map/ppermute | solution.py:32
  203.7 4.4 %collective-permute-done.33 = f32[3,1,16,128]{3,2,1,0:T(8,128)S(1)} collective-permute-done((f32[3,1,16,128]{3,2,1,0:T(8,128)S(1)}, f32[3,1,16,128]{3,2,1,0:T(8,128)S(1)}, u32[]{:S(2)}, u32[]{:S(2)}) %collective-permute-start.33) | collective-permute-done | bytes 24608 | tf_op jit(solution)/shard_map/ppermute | solution.py:33
  208.9 2.2 collective-permute-start.34
  213.4 3.9 %collective-permute-done.35 = f32[3,34,16,1]{1,2,3,0:T(8,128)S(1)} collective-permute-done((f32[3,34,16,1]{1,2,3,0:T(8,128)S(1)}, f32[3,34,16,1]{1,2,3,0:T(8,128)S(1)}, u32[]{:S(2)}, u32[]{:S(2)}) %collective-permute-start.35) | collective-permute-done | bytes 6560 | tf_op jit(solution)/shard_map/ppermute | solution.py:33
  221.2 13.2 %all_to_all.14 = bf16[2,6,32,8,128]{4,3,2,1,0:T(8,128)(2,1)S(1)} all-to-all(bf16[2,6,32,8,128]{4,3,2,1,0:T(8,128)(2,1)S(1)} %pad_maximum_fusion.15), channel_id=1, replica_groups=mesh['gx'=4,'gy'=2,'gz'=4] {'gy'}, dimensions={0} | all-to-all | bytes 1572864 | tf_op jit(solution)/shard_map/all_to_all | solution.py:15
  (164 shorter events, 70.4 us)
Async XLA Ops:
  2.0 17.3 %copy-start = (bf16[3,64,8,128]{3,2,1,0:T(8,128)(2,1)}, bf16[3,64,8,128]{3,2,1,0:T(8,128)(2,1)S(1)}, u32[]{:S(2)}) copy-start(bf16[3,64,8,128]{3,2,1,0:T(8,128)(2,1)S(1)} %broadcast_multiply_fusion) | copy-start | bytes 1179652
  2.0 3.7 %collective-permute-start = (bf16[3,1,8,128]{3,2,1,0:T(8,128)(2,1)S(1)}, bf16[3,1,8,128]{3,2,1,0:T(8,128)(2,1)S(1)}, u32[]{:S(2)}, u32[]{:S(2)}) collective-permute-start(bf16[3,1,8,128]{3,2,1,0:T(8,128)(2,1)S(1)} %get-tuple-element.56), channel_id=1, source_target_pairs={{0,8},{8,16},{16,24},{1,9},{9,17},{17,25},{2,10},{10,18},{18,26},{... | collective-permute-start | bytes 18440 | tf_op jit(solution)/shard_map/ppermute | solution.py:32
  4.4 5.2 %collective-permute-start.1 = (bf16[3,1,8,128]{3,2,1,0:T(8,128)(2,1)S(1)}, bf16[3,1,8,128]{3,2,1,0:T(8,128)(2,1)S(1)}, u32[]{:S(2)}, u32[]{:S(2)}) collective-permute-start(bf16[3,1,8,128]{3,2,1,0:T(8,128)(2,1)S(1)} %get-tuple-element.57), channel_id=1, source_target_pairs={{8,0},{16,8},{24,16},{9,1},{17,9},{25,17},{10,2},{18,10},{26,18},{... | collective-permute-start | bytes 18440 | tf_op jit(solution)/shard_map/ppermute | solution.py:33
  9.7 5.2 %collective-permute-start.2 = (bf16[3,66,1,128]{3,1,2,0:T(8,128)(2,1)S(1)}, bf16[3,66,1,128]{3,1,2,0:T(8,128)(2,1)S(1)}, u32[]{:S(2)}, u32[]{:S(2)}) collective-permute-start(bf16[3,66,1,128]{3,1,2,0:T(8,128)(2,1)S(1)} %copy.120), channel_id=1, source_target_pairs={{0,4},{1,5},{2,6},{3,7},{8,12},{9,13},{10,14},{11,15},{16,20},{17,... | collective-permute-start | bytes 152072 | tf_op jit(solution)/shard_map/ppermute | solution.py:32
  13.2 6.0 %collective-permute-start.3 = (bf16[3,66,1,128]{3,1,2,0:T(8,128)(2,1)S(1)}, bf16[3,66,1,128]{3,1,2,0:T(8,128)(2,1)S(1)}, u32[]{:S(2)}, u32[]{:S(2)}) collective-permute-start(bf16[3,66,1,128]{3,1,2,0:T(8,128)(2,1)S(1)} %copy.121), channel_id=1, source_target_pairs={{4,0},{5,1},{6,2},{7,3},{12,8},{13,9},{14,10},{15,11},{20,16},{21,... | collective-permute-start | bytes 152072 | tf_op jit(solution)/shard_map/ppermute | solution.py:33
  21.0 5.5 %collective-permute-start.4 = (bf16[3,66,10,1]{1,2,3,0:T(8,128)(2,1)S(1)}, bf16[3,66,10,1]{1,2,3,0:T(8,128)(2,1)S(1)}, u32[]{:S(2)}, u32[]{:S(2)}) collective-permute-start(bf16[3,66,10,1]{1,2,3,0:T(8,128)(2,1)S(1)} %copy.124), channel_id=1, source_target_pairs={{0,1},{1,2},{2,3},{4,5},{5,6},{6,7},{8,9},{9,10},{10,11},{12,13},{... | collective-permute-start | bytes 11888 | tf_op jit(solution)/shard_map/ppermute | solution.py:32
  25.2 5.6 %collective-permute-start.5 = (bf16[3,66,10,1]{1,2,3,0:T(8,128)(2,1)S(1)}, bf16[3,66,10,1]{1,2,3,0:T(8,128)(2,1)S(1)}, u32[]{:S(2)}, u32[]{:S(2)}) collective-permute-start(bf16[3,66,10,1]{1,2,3,0:T(8,128)(2,1)S(1)} %copy.125), channel_id=1, source_target_pairs={{1,0},{2,1},{3,2},{5,4},{6,5},{7,6},{9,8},{10,9},{11,10},{13,12},{... | collective-permute-start | bytes 11888 | tf_op jit(solution)/shard_map/ppermute | solution.py:33
  37.7 4.3 %collective-permute-start.6 = (f32[2,8,128]{2,1,0:T(8,128)S(1)}, f32[2,8,128]{2,1,0:T(8,128)S(1)}, u32[]{:S(2)}, u32[]{:S(2)}) collective-permute-start(f32[2,8,128]{2,1,0:T(8,128)S(1)} %get-tuple-element.69), channel_id=1, source_target_pairs={{8,0},{16,8},{24,16},{9,1},{17,9},{25,17},{10,2},{18,10},{26,18},{... | collective-permute-start | bytes 24584 | tf_op jit(solution)/shard_map/ppermute | solution.py:33
  39.0 3.8 %collective-permute-start.7 = (f32[2,8,128]{2,1,0:T(8,128)S(1)}, f32[2,8,128]{2,1,0:T(8,128)S(1)}, u32[]{:S(2)}, u32[]{:S(2)}) collective-permute-start(f32[2,8,128]{2,1,0:T(8,128)S(1)} %get-tuple-element.68), channel_id=1, source_target_pairs={{0,8},{8,16},{16,24},{1,9},{9,17},{17,25},{2,10},{10,18},{18,26},{... | collective-permute-start | bytes 24584 | tf_op jit(solution)/shard_map/ppermute | solution.py:32
  42.9 6.2 %collective-permute-start.8 = (f32[68,2,128]{2,1,0:T(2,128)S(1)}, f32[68,2,128]{2,1,0:T(2,128)S(1)}, u32[]{:S(2)}, u32[]{:S(2)}) collective-permute-start(f32[68,2,128]{2,1,0:T(2,128)S(1)} %get-tuple-element.63), channel_id=1, source_target_pairs={{4,0},{5,1},{6,2},{7,3},{12,8},{13,9},{14,10},{15,11},{20,16},{21,... | collective-permute-start | bytes 208904 | tf_op jit(solution)/shard_map/ppermute | solution.py:33
  44.2 6.5 %collective-permute-start.9 = (f32[68,2,128]{2,1,0:T(2,128)S(1)}, f32[68,2,128]{2,1,0:T(2,128)S(1)}, u32[]{:S(2)}, u32[]{:S(2)}) collective-permute-start(f32[68,2,128]{2,1,0:T(2,128)S(1)} %get-tuple-element.62), channel_id=1, source_target_pairs={{0,4},{1,5},{2,6},{3,7},{8,12},{9,13},{10,14},{11,15},{16,20},{17,... | collective-permute-start | bytes 208904 | tf_op jit(solution)/shard_map/ppermute | solution.py:32
  49.1 1.6 copy-start.17
  53.9 8.3 %collective-permute-start.10 = (f32[68,12,2]{0,2,1:T(2,128)S(1)}, f32[68,12,2]{0,2,1:T(2,128)S(1)}, u32[]{:S(2)}, u32[]{:S(2)}) collective-permute-start(f32[68,12,2]{0,2,1:T(2,128)S(1)} %copy.128), channel_id=1, source_target_pairs={{1,0},{2,1},{3,2},{5,4},{6,5},{7,6},{9,8},{10,9},{11,10},{13,12},{... | collective-permute-start | bytes 19592 | tf_op jit(solution)/shard_map/ppermute | solution.py:33
  57.1 6.3 %collective-permute-start.11 = (f32[68,12,2]{0,2,1:T(2,128)}, f32[68,12,2]{0,2,1:T(2,128)}, u32[]{:S(2)}, u32[]{:S(2)}) collective-permute-start(f32[68,12,2]{0,2,1:T(2,128)} %copy.130), channel_id=1, source_target_pairs={{0,1},{1,2},{2,3},{4,5},{5,6},{6,7},{8,9},{9,10},{10,11},{12,13},{... | collective-permute-start | bytes 19592 | tf_op jit(solution)/shard_map/ppermute | solution.py:32
  67.2 14.9 %copy-start.3 = (f32[64,8,128]{2,1,0:T(8,128)}, f32[64,8,128]{2,1,0:T(8,128)S(1)}, u32[]{:S(2)}) copy-start(f32[64,8,128]{2,1,0:T(8,128)S(1)} %fusion.113) | copy-start | bytes 786436
  67.2 4.3 %collective-permute-start.12 = (f32[2,8,128]{2,1,0:T(8,128)S(1)}, f32[2,8,128]{2,1,0:T(8,128)S(1)}, u32[]{:S(2)}, u32[]{:S(2)}) collective-permute-start(f32[2,8,128]{2,1,0:T(8,128)S(1)} %get-tuple-element.67), channel_id=1, source_target_pairs={{8,0},{16,8},{24,16},{9,1},{17,9},{25,17},{10,2},{18,10},{26,18},{... | collective-permute-start | bytes 24584 | tf_op jit(solution)/shard_map/ppermute | solution.py:33
  68.5 3.8 %collective-permute-start.13 = (f32[2,8,128]{2,1,0:T(8,128)S(1)}, f32[2,8,128]{2,1,0:T(8,128)S(1)}, u32[]{:S(2)}, u32[]{:S(2)}) collective-permute-start(f32[2,8,128]{2,1,0:T(8,128)S(1)} %get-tuple-element.66), channel_id=1, source_target_pairs={{0,8},{8,16},{16,24},{1,9},{9,17},{17,25},{2,10},{10,18},{18,26},{... | collective-permute-start | bytes 24584 | tf_op jit(solution)/shard_map/ppermute | solution.py:32
  72.4 6.2 %collective-permute-start.14 = (f32[68,2,128]{2,1,0:T(2,128)S(1)}, f32[68,2,128]{2,1,0:T(2,128)S(1)}, u32[]{:S(2)}, u32[]{:S(2)}) collective-permute-start(f32[68,2,128]{2,1,0:T(2,128)S(1)} %get-tuple-element.61), channel_id=1, source_target_pairs={{4,0},{5,1},{6,2},{7,3},{12,8},{13,9},{14,10},{15,11},{20,16},{21,... | collective-permute-start | bytes 208904 | tf_op jit(solution)/shard_map/ppermute | solution.py:33
  73.7 6.5 %collective-permute-start.15 = (f32[68,2,128]{2,1,0:T(2,128)S(1)}, f32[68,2,128]{2,1,0:T(2,128)S(1)}, u32[]{:S(2)}, u32[]{:S(2)}) collective-permute-start(f32[68,2,128]{2,1,0:T(2,128)S(1)} %get-tuple-element.60), channel_id=1, source_target_pairs={{0,4},{1,5},{2,6},{3,7},{8,12},{9,13},{10,14},{11,15},{16,20},{17,... | collective-permute-start | bytes 208904 | tf_op jit(solution)/shard_map/ppermute | solution.py:32
  78.6 1.6 copy-start.18
  83.3 7.4 %collective-permute-start.16 = (f32[68,12,2]{0,2,1:T(2,128)S(1)}, f32[68,12,2]{0,2,1:T(2,128)S(1)}, u32[]{:S(2)}, u32[]{:S(2)}) collective-permute-start(f32[68,12,2]{0,2,1:T(2,128)S(1)} %copy.132), channel_id=1, source_target_pairs={{1,0},{2,1},{3,2},{5,4},{6,5},{7,6},{9,8},{10,9},{11,10},{13,12},{... | collective-permute-start | bytes 19592 | tf_op jit(solution)/shard_map/ppermute | solution.py:33
  85.9 6.2 %collective-permute-start.17 = (f32[68,12,2]{0,2,1:T(2,128)S(1)}, f32[68,12,2]{0,2,1:T(2,128)S(1)}, u32[]{:S(2)}, u32[]{:S(2)}) collective-permute-start(f32[68,12,2]{0,2,1:T(2,128)S(1)} %copy.134), channel_id=1, source_target_pairs={{0,1},{1,2},{2,3},{4,5},{5,6},{6,7},{8,9},{9,10},{10,11},{12,13},{... | collective-permute-start | bytes 19592 | tf_op jit(solution)/shard_map/ppermute | solution.py:32
  95.9 5.2 %collective-permute-start.18 = (f32[2,8,128]{2,1,0:T(8,128)S(1)}, f32[2,8,128]{2,1,0:T(8,128)S(1)}, u32[]{:S(2)}, u32[]{:S(2)}) collective-permute-start(f32[2,8,128]{2,1,0:T(8,128)S(1)} %get-tuple-element.64), channel_id=1, source_target_pairs={{0,8},{8,16},{16,24},{1,9},{9,17},{17,25},{2,10},{10,18},{18,26},{... | collective-permute-start | bytes 24584 | tf_op jit(solution)/shard_map/ppermute | solution.py:32
  99.8 6.5 %collective-permute-start.19 = (f32[2,8,128]{2,1,0:T(8,128)S(1)}, f32[2,8,128]{2,1,0:T(8,128)S(1)}, u32[]{:S(2)}, u32[]{:S(2)}) collective-permute-start(f32[2,8,128]{2,1,0:T(8,128)S(1)} %get-tuple-element.65), channel_id=1, source_target_pairs={{8,0},{16,8},{24,16},{9,1},{17,9},{25,17},{10,2},{18,10},{26,18},{... | collective-permute-start | bytes 24584 | tf_op jit(solution)/shard_map/ppermute | solution.py:33
  106.3 6.2 %collective-permute-start.20 = (f32[68,2,128]{2,1,0:T(2,128)S(1)}, f32[68,2,128]{2,1,0:T(2,128)S(1)}, u32[]{:S(2)}, u32[]{:S(2)}) collective-permute-start(f32[68,2,128]{2,1,0:T(2,128)S(1)} %get-tuple-element.58), channel_id=1, source_target_pairs={{0,4},{1,5},{2,6},{3,7},{8,12},{9,13},{10,14},{11,15},{16,20},{17,... | collective-permute-start | bytes 208904 | tf_op jit(solution)/shard_map/ppermute | solution.py:32
  110.6 6.2 %collective-permute-start.21 = (f32[68,2,128]{2,1,0:T(2,128)S(1)}, f32[68,2,128]{2,1,0:T(2,128)S(1)}, u32[]{:S(2)}, u32[]{:S(2)}) collective-permute-start(f32[68,2,128]{2,1,0:T(2,128)S(1)} %get-tuple-element.59), channel_id=1, source_target_pairs={{4,0},{5,1},{6,2},{7,3},{12,8},{13,9},{14,10},{15,11},{20,16},{21,... | collective-permute-start | bytes 208904 | tf_op jit(solution)/shard_map/ppermute | solution.py:33
  112.5 4.3 %copy-start.13 = (f32[68,2,128]{2,1,0:T(2,128)}, f32[68,2,128]{2,1,0:T(2,128)S(1)}, u32[]{:S(2)}) copy-start(f32[68,2,128]{2,1,0:T(2,128)S(1)} %collective-permute-done.20) | copy-start | bytes 208900
  120.0 7.5 %collective-permute-start.22 = (f32[68,12,2]{0,2,1:T(2,128)S(1)}, f32[68,12,2]{0,2,1:T(2,128)S(1)}, u32[]{:S(2)}, u32[]{:S(2)}) collective-permute-start(f32[68,12,2]{0,2,1:T(2,128)S(1)} %copy.136), channel_id=1, source_target_pairs={{0,1},{1,2},{2,3},{4,5},{5,6},{6,7},{8,9},{9,10},{10,11},{12,13},{... | collective-permute-start | bytes 19592 | tf_op jit(solution)/shard_map/ppermute | solution.py:32
  126.0 6.0 %collective-permute-start.23 = (f32[68,12,2]{0,2,1:T(2,128)}, f32[68,12,2]{0,2,1:T(2,128)}, u32[]{:S(2)}, u32[]{:S(2)}) collective-permute-start(f32[68,12,2]{0,2,1:T(2,128)} %copy.137), channel_id=1, source_target_pairs={{1,0},{2,1},{3,2},{5,4},{6,5},{7,6},{9,8},{10,9},{11,10},{13,12},{... | collective-permute-start | bytes 19592 | tf_op jit(solution)/shard_map/ppermute | solution.py:33
  133.9 2.2 copy-start.1
  133.9 2.2 copy-start.2
  133.9 2.2 copy-start.14
  133.9 2.2 copy-start.16
  141.2 4.4 %copy-start.10 = (f32[32,16,128]{2,1,0:T(8,128)S(1)}, f32[32,16,128]{2,1,0:T(8,128)}, u32[]{:S(2)}) copy-start(f32[32,16,128]{2,1,0:T(8,128)} %param.7) | copy-start | bytes 786436
  142.0 10.6 %all-to-all-start = ((bf16[3,64,8,128]{3,2,0,1:T(8,128)(2,1)}), bf16[3,64,8,128]{3,2,0,1:T(8,128)(2,1)S(1)}, u32[]{:S(2)}, u32[]{:S(2)}) async-start(bf16[3,64,8,128]{3,2,0,1:T(8,128)(2,1)} %copy.142), calls=%async_computation | async-start | bytes 786432 | tf_op jit(solution)/shard_map/all_to_all | solution.py:174
  152.7 3.7 %collective-permute-start.24 = (f32[3,1,16,128]{3,2,1,0:T(8,128)S(1)}, f32[3,1,16,128]{3,2,1,0:T(8,128)S(1)}, u32[]{:S(2)}, u32[]{:S(2)}) collective-permute-start(f32[3,1,16,128]{3,2,1,0:T(8,128)S(1)} %get-tuple-element.46), channel_id=1, source_target_pairs={{0,4},{4,8},{8,12},{12,16},{16,20},{20,24},{24,28},{1,5},{5,9},{9,... | collective-permute-start | bytes 73736 | tf_op jit(solution)/shard_map/ppermute | solution.py:32
  154.9 5.7 %collective-permute-start.25 = (f32[3,1,16,128]{3,2,1,0:T(8,128)S(1)}, f32[3,1,16,128]{3,2,1,0:T(8,128)S(1)}, u32[]{:S(2)}, u32[]{:S(2)}) collective-permute-start(f32[3,1,16,128]{3,2,1,0:T(8,128)S(1)} %get-tuple-element.47), channel_id=1, source_target_pairs={{4,0},{8,4},{12,8},{16,12},{20,16},{24,20},{28,24},{5,1},{9,5},{13... | collective-permute-start | bytes 73736 | tf_op jit(solution)/shard_map/ppermute | solution.py:33
  161.5 5.0 %collective-permute-start.26 = (f32[3,34,16,1]{1,2,3,0:T(8,128)S(1)}, f32[3,34,16,1]{1,2,3,0:T(8,128)S(1)}, u32[]{:S(2)}, u32[]{:S(2)}) collective-permute-start(f32[3,34,16,1]{1,2,3,0:T(8,128)S(1)} %copy.157), channel_id=1, source_target_pairs={{0,1},{1,2},{2,3},{4,5},{5,6},{6,7},{8,9},{9,10},{10,11},{12,13},{... | collective-permute-start | bytes 19592 | tf_op jit(solution)/shard_map/ppermute | solution.py:32
  165.2 5.7 %collective-permute-start.27 = (f32[3,34,16,1]{1,2,3,0:T(8,128)S(1)}, f32[3,34,16,1]{1,2,3,0:T(8,128)S(1)}, u32[]{:S(2)}, u32[]{:S(2)}) collective-permute-start(f32[3,34,16,1]{1,2,3,0:T(8,128)S(1)} %copy.158), channel_id=1, source_target_pairs={{1,0},{2,1},{3,2},{5,4},{6,5},{7,6},{9,8},{10,9},{11,10},{13,12},{... | collective-permute-start | bytes 19592 | tf_op jit(solution)/shard_map/ppermute | solution.py:33
  176.3 3.1 %collective-permute-start.28 = (f32[3,1,16,128]{3,2,1,0:T(8,128)S(1)}, f32[3,1,16,128]{3,2,1,0:T(8,128)S(1)}, u32[]{:S(2)}, u32[]{:S(2)}) collective-permute-start(f32[3,1,16,128]{3,2,1,0:T(8,128)S(1)} %get-tuple-element.44), channel_id=1, source_target_pairs={{0,4},{4,8},{8,12},{12,16},{16,20},{20,24},{24,28},{1,5},{5,9},{9,... | collective-permute-start | bytes 73736 | tf_op jit(solution)/shard_map/ppermute | solution.py:32
  177.9 5.7 %collective-permute-start.29 = (f32[3,1,16,128]{3,2,1,0:T(8,128)S(1)}, f32[3,1,16,128]{3,2,1,0:T(8,128)S(1)}, u32[]{:S(2)}, u32[]{:S(2)}) collective-permute-start(f32[3,1,16,128]{3,2,1,0:T(8,128)S(1)} %get-tuple-element.45), channel_id=1, source_target_pairs={{4,0},{8,4},{12,8},{16,12},{20,16},{24,20},{28,24},{5,1},{9,5},{13... | collective-permute-start | bytes 73736 | tf_op jit(solution)/shard_map/ppermute | solution.py:33
  184.4 5.2 %collective-permute-start.30 = (f32[3,34,16,1]{1,2,3,0:T(8,128)S(1)}, f32[3,34,16,1]{1,2,3,0:T(8,128)S(1)}, u32[]{:S(2)}, u32[]{:S(2)}) collective-permute-start(f32[3,34,16,1]{1,2,3,0:T(8,128)S(1)} %copy.159), channel_id=1, source_target_pairs={{0,1},{1,2},{2,3},{4,5},{5,6},{6,7},{8,9},{9,10},{10,11},{12,13},{... | collective-permute-start | bytes 19592 | tf_op jit(solution)/shard_map/ppermute | solution.py:32
  188.3 5.7 %collective-permute-start.31 = (f32[3,34,16,1]{1,2,3,0:T(8,128)S(1)}, f32[3,34,16,1]{1,2,3,0:T(8,128)S(1)}, u32[]{:S(2)}, u32[]{:S(2)}) collective-permute-start(f32[3,34,16,1]{1,2,3,0:T(8,128)S(1)} %copy.160), channel_id=1, source_target_pairs={{1,0},{2,1},{3,2},{5,4},{6,5},{7,6},{9,8},{10,9},{11,10},{13,12},{... | collective-permute-start | bytes 19592 | tf_op jit(solution)/shard_map/ppermute | solution.py:33
  197.7 1.1 copy-start.12
  199.1 4.6 %collective-permute-start.32 = (f32[3,1,16,128]{3,2,1,0:T(8,128)S(1)}, f32[3,1,16,128]{3,2,1,0:T(8,128)S(1)}, u32[]{:S(2)}, u32[]{:S(2)}) collective-permute-start(f32[3,1,16,128]{3,2,1,0:T(8,128)S(1)} %get-tuple-element.42), channel_id=1, source_target_pairs={{0,4},{4,8},{8,12},{12,16},{16,20},{20,24},{24,28},{1,5},{5,9},{9,... | collective-permute-start | bytes 73736 | tf_op jit(solution)/shard_map/ppermute | solution.py:32
  202.2 5.9 %collective-permute-start.33 = (f32[3,1,16,128]{3,2,1,0:T(8,128)S(1)}, f32[3,1,16,128]{3,2,1,0:T(8,128)S(1)}, u32[]{:S(2)}, u32[]{:S(2)}) collective-permute-start(f32[3,1,16,128]{3,2,1,0:T(8,128)S(1)} %get-tuple-element.43), channel_id=1, source_target_pairs={{4,0},{8,4},{12,8},{16,12},{20,16},{24,20},{28,24},{5,1},{9,5},{13... | collective-permute-start | bytes 73736 | tf_op jit(solution)/shard_map/ppermute | solution.py:33
  208.9 3.9 %collective-permute-start.34 = (f32[3,34,16,1]{1,2,3,0:T(8,128)S(1)}, f32[3,34,16,1]{1,2,3,0:T(8,128)S(1)}, u32[]{:S(2)}, u32[]{:S(2)}) collective-permute-start(f32[3,34,16,1]{1,2,3,0:T(8,128)S(1)} %copy.161), channel_id=1, source_target_pairs={{0,1},{1,2},{2,3},{4,5},{5,6},{6,7},{8,9},{9,10},{10,11},{12,13},{... | collective-permute-start | bytes 19592 | tf_op jit(solution)/shard_map/ppermute | solution.py:32
  211.6 5.7 %collective-permute-start.35 = (f32[3,34,16,1]{1,2,3,0:T(8,128)S(1)}, f32[3,34,16,1]{1,2,3,0:T(8,128)S(1)}, u32[]{:S(2)}, u32[]{:S(2)}) collective-permute-start(f32[3,34,16,1]{1,2,3,0:T(8,128)S(1)} %copy.162), channel_id=1, source_target_pairs={{1,0},{2,1},{3,2},{5,4},{6,5},{7,6},{9,8},{10,9},{11,10},{13,12},{... | collective-permute-start | bytes 19592 | tf_op jit(solution)/shard_map/ppermute | solution.py:33
  (10 other events, 8.3 us)
